TPU v7x, 32 devices: a whole 2x2x4 slice. The times are simulated.
32 devices in a mesh: groups: 2 (over y), beam: 16 (over z, x, core).
Axes of the slice: x: 2, y: 2, z: 4, core: 2. Of those that a mesh axis runs over, the one named last changes fastest.
Arguments:
- potential: float32 [4, 512, 512], P('groups', 'beam'), parts along dimension 0, may hold values from -5 to 5
- beam_tilts: int32 [16, 2], replicated, may hold values from -16 to 16
- aperture: float32 [16], replicated, may hold values from 0.3 to 3
- aberration: float32 [16], replicated, may hold values from -3.140625 to 3.140625
- probe_spots: int32 [8, 32, 2], P('groups'), parts along dimension 0, may hold values from 0 to 127
- crop_anchor: int32 [4], P('groups'), parts along dimension 0, may hold values from 0 to 256
Outputs:
- diffraction: float32 [1024, 32, 128], P(('groups', 'beam')), parts along dimension 0
There are 2 independent parts, one for each index of `groups`. A program takes and returns all parts, laid end to end along the dimension named above; an argument that names none is the same for every part. Nothing has to cross between parts.
Inputs may be any that keep to these rules, and one draw needn't show every extreme that they name: `probe_spots`: positions inside a tile. `crop_anchor`: the window lies inside the grid.
All inputs are finite; a program needn't handle non-finite values.
Results may differ from a plain program's by a relative error of at most 0.0003.
Values sent between devices are 32-bit elements; how exact they have to be, the bound alone decides.
A program may use at most 64 MiB of HBM per device.

v0:
```python
import jax
import jax.numpy as jnp
from jax import lax
from jax.sharding import PartitionSpec as P

CROP = 256
TILE = 128


precise = lax.Precision.HIGHEST


def dft_factors(row_count, col_count, period, direction):
    product = (
        jnp.arange(row_count, dtype=jnp.int32)[:, None]
        * jnp.arange(col_count, dtype=jnp.int32)[None, :]
    )
    phase_angle = 2.0 * jnp.pi / period * jnp.remainder(product, period).astype(jnp.float32)
    return (jnp.cos(phase_angle), direction * jnp.sin(phase_angle))


def complex_einsum(formula, left_real, left_imag, right_real, right_imag):
    real_real = jnp.einsum(formula, left_real, right_real, precision=precise)
    imag_imag = jnp.einsum(formula, left_imag, right_imag, precision=precise)
    real_imag = jnp.einsum(formula, left_real, right_imag, precision=precise)
    imag_real = jnp.einsum(formula, left_imag, right_real, precision=precise)
    return (real_real - imag_imag, real_imag + imag_real)


def twiddle(values_real, values_imag, table_real, table_imag):
    return (
        values_real * table_real - values_imag * table_imag,
        values_real * table_imag + values_imag * table_real,
    )


def rows_forward(field_real, field_imag):
    length, breadth = field_real.shape
    inner_size = length // 32
    blocks_real = field_real.reshape(32, inner_size, breadth)
    blocks_imag = field_imag.reshape(32, inner_size, breadth)
    first_real, first_imag = dft_factors(32, 32, 32, -1.0)
    part_real, part_imag = complex_einsum(
        "mnc,mj->jnc", blocks_real, blocks_imag, first_real, first_imag
    )
    turn_real, turn_imag = dft_factors(32, inner_size, length, -1.0)
    part_real, part_imag = twiddle(
        part_real, part_imag, turn_real[:, :, None], turn_imag[:, :, None]
    )
    second_real, second_imag = dft_factors(inner_size, inner_size, inner_size, -1.0)
    done_real, done_imag = complex_einsum(
        "jnc,nk->kjc", part_real, part_imag, second_real, second_imag
    )
    return (done_real.reshape(length, breadth), done_imag.reshape(length, breadth))


def rows_inverse(field_real, field_imag):
    length, breadth = field_real.shape
    inner_size = length // 32
    blocks_real = field_real.reshape(inner_size, 32, breadth)
    blocks_imag = field_imag.reshape(inner_size, 32, breadth)
    first_real, first_imag = dft_factors(inner_size, inner_size, inner_size, 1.0)
    part_real, part_imag = complex_einsum(
        "kjc,kn->njc", blocks_real, blocks_imag, first_real, first_imag
    )
    turn_real, turn_imag = dft_factors(inner_size, 32, length, 1.0)
    part_real, part_imag = twiddle(
        part_real, part_imag, turn_real[:, :, None], turn_imag[:, :, None]
    )
    second_real, second_imag = dft_factors(32, 32, 32, 1.0)
    done_real, done_imag = complex_einsum(
        "njc,jm->mnc", part_real, part_imag, second_real, second_imag
    )
    inverse_scale = 1.0 / length
    return (
        done_real.reshape(length, breadth) * inverse_scale,
        done_imag.reshape(length, breadth) * inverse_scale,
    )


def cols_forward(field_real, field_imag):
    height, length = field_real.shape
    inner_size = length // 8
    blocks_real = field_real.reshape(height, 8, inner_size)
    blocks_imag = field_imag.reshape(height, 8, inner_size)
    first_real, first_imag = dft_factors(8, 8, 8, -1.0)
    part_real, part_imag = complex_einsum(
        "rmn,mj->rjn", blocks_real, blocks_imag, first_real, first_imag
    )
    turn_real, turn_imag = dft_factors(8, inner_size, length, -1.0)
    part_real, part_imag = twiddle(part_real, part_imag, turn_real[None], turn_imag[None])
    second_real, second_imag = dft_factors(inner_size, inner_size, inner_size, -1.0)
    return complex_einsum("rjn,nk->rjk", part_real, part_imag, second_real, second_imag)


def cols_inverse(spec_real, spec_imag):
    height = spec_real.shape[0]
    inner_size = spec_real.shape[2]
    length = 8 * inner_size
    first_real, first_imag = dft_factors(inner_size, inner_size, inner_size, 1.0)
    part_real, part_imag = complex_einsum(
        "rjk,kn->rjn", spec_real, spec_imag, first_real, first_imag
    )
    turn_real, turn_imag = dft_factors(8, inner_size, length, 1.0)
    part_real, part_imag = twiddle(part_real, part_imag, turn_real[None], turn_imag[None])
    second_real, second_imag = dft_factors(8, 8, 8, 1.0)
    done_real, done_imag = complex_einsum(
        "rjn,jm->rmn", part_real, part_imag, second_real, second_imag
    )
    inverse_scale = 1.0 / length
    return (
        done_real.reshape(height, length) * inverse_scale,
        done_imag.reshape(height, length) * inverse_scale,
    )


def propagator_table(length):
    inner_size = length // 8
    index_rows = jnp.arange(length, dtype=jnp.int32)
    freq_rows = jnp.where(index_rows < length // 2, index_rows, index_rows - length)
    index_cols = (
        jnp.arange(8, dtype=jnp.int32)[:, None]
        + 8 * jnp.arange(inner_size, dtype=jnp.int32)[None, :]
    )
    freq_cols = jnp.where(index_cols < length // 2, index_cols, index_cols - length)
    square = freq_rows[:, None, None] ** 2 + freq_cols[None, :, :] ** 2
    phase_angle = jnp.pi / length * jnp.remainder(square, 2 * length).astype(jnp.float32)
    passing = 9 * square < length * length
    return (
        jnp.where(passing, jnp.cos(phase_angle), 0.0),
        jnp.where(passing, -jnp.sin(phase_angle), 0.0),
    )


def per_device(potential, beam_tilts, aperture, aberration, probe_spots, crop_anchor):
    layer_count = potential.shape[0]
    length = potential.shape[2]
    device = lax.axis_index("beam")
    own_tilt = lax.dynamic_slice_in_dim(beam_tilts, device, 1, 0)
    coords = jnp.arange(length, dtype=jnp.int32)
    plane_phase = jnp.remainder(
        own_tilt[0, 0] * coords[:, None] + own_tilt[0, 1] * coords[None, :], length
    )
    plane_angle = 2.0 * jnp.pi / length * plane_phase.astype(jnp.float32)
    wave_real = jnp.cos(plane_angle)
    wave_imag = jnp.sin(plane_angle)
    pass_real, pass_imag = propagator_table(length)
    for layer_index in range(layer_count):
        full_slice = lax.all_gather(potential[layer_index], "beam", axis=0, tiled=True)
        trans_real = jnp.cos(full_slice)
        trans_imag = jnp.sin(full_slice)
        wave_real, wave_imag = twiddle(wave_real, wave_imag, trans_real, trans_imag)
        if layer_index + 1 < layer_count:
            wave_real, wave_imag = rows_forward(wave_real, wave_imag)
            spec_real, spec_imag = cols_forward(wave_real, wave_imag)
            spec_real, spec_imag = twiddle(spec_real, spec_imag, pass_real, pass_imag)
            wave_real, wave_imag = cols_inverse(spec_real, spec_imag)
            wave_real, wave_imag = rows_inverse(wave_real, wave_imag)
    per_side = CROP // TILE
    crop_real = lax.dynamic_slice(
        wave_real, (crop_anchor[0], crop_anchor[1]), (CROP, CROP)
    ).reshape(per_side, TILE, per_side, TILE)
    crop_imag = lax.dynamic_slice(
        wave_imag, (crop_anchor[0], crop_anchor[1]), (CROP, CROP)
    ).reshape(per_side, TILE, per_side, TILE)
    tile_real, tile_imag = dft_factors(TILE, TILE, TILE, -1.0)
    part_real, part_imag = complex_einsum(
        "aybx,xk->aybk", crop_real, crop_imag, tile_real, tile_imag
    )
    spec_real, spec_imag = complex_einsum(
        "aybk,yj->abjk", part_real, part_imag, tile_real, tile_imag
    )
    tile_count = per_side * per_side
    payload = jnp.stack(
        (spec_real.reshape(tile_count * TILE, TILE), spec_imag.reshape(tile_count * TILE, TILE))
    )[:, None]
    arrived = lax.all_to_all(payload, "beam", split_axis=2, concat_axis=1, tiled=True)
    rows_here = arrived.shape[2]
    my_tile = device * rows_here // TILE
    probe_here = lax.dynamic_slice_in_dim(probe_spots, my_tile, 1, 0)[0]
    anchor_rows = crop_anchor[0] + TILE * (my_tile // per_side)
    anchor_cols = crop_anchor[1] + TILE * (my_tile % per_side)
    spot_rows = anchor_rows + probe_here[:, 0]
    spot_cols = anchor_cols + probe_here[:, 1]
    phase_index = jnp.remainder(
        spot_rows[:, None] * beam_tilts[None, :, 0] + spot_cols[:, None] * beam_tilts[None, :, 1],
        length,
    )
    weight_angle = aberration[None, :] - 2.0 * jnp.pi / length * phase_index.astype(jnp.float32)
    weight_real = aperture[None, :] * jnp.cos(weight_angle)
    weight_imag = aperture[None, :] * jnp.sin(weight_angle)
    exit_real, exit_imag = complex_einsum(
        "pb,brk->rpk", weight_real, weight_imag, arrived[0], arrived[1]
    )
    intensity = exit_real * exit_real + exit_imag * exit_imag
    partial_sums = jnp.sum(intensity, axis=(0, 2))
    tile_slots = jnp.where(
        jnp.arange(tile_count, dtype=jnp.int32)[:, None] == my_tile, partial_sums[None, :], 0.0
    )
    totals = lax.psum(tile_slots, "beam")
    own_total = lax.dynamic_slice_in_dim(totals, my_tile, 1, 0)[0]
    mean_level = own_total / (TILE * TILE)
    return intensity / (mean_level[None, :, None] + 1e-06)


def solution(mesh):
    placed = (P("groups", "beam", None), P(), P(), P(), P("groups", None, None), P("groups"))
    return jax.shard_map(
        per_device,
        mesh=mesh,
        in_specs=placed,
        out_specs=P(("groups", "beam"), None, None),
        check_vma=False,
    )
```

profile of v0, /device:TPU:0, one launch (start us, length us, event | category | flops | bytes accessed | tf_op | source)
XLA Modules:
  0.0 222.5 jit_solution(5073884342935992165)
XLA Ops:
  6.5 1.5 fusion.447
  9.1 1.3 fusion.449
  14.5 1.3 iota_multiply_fusion
  17.0 33.2 %all-gather.5.cloned.1.call-done = f32[1,512,512]{2,1,0:T(8,128)} async-done(((f32[1,32,512]{2,1,0:T(8,128)}), f32[1,512,512]{2,1,0:T(8,128)}) %all-gather.5.cloned.1.call-update) | async-done | bytes 1048592 | tf_op jit(solution)/shard_map/all_gather | solution.py:149
  50.2 4.7 %fusion.445 = (f32[1,512,512]{2,1,0:T(8,128)S(1)}, f32[1,512,512]{2,1,0:T(8,128)S(1)}) fusion(f32[1,512,512]{2,1,0:T(8,128)} %all-gather.5.cloned.1.call-done), kind=kLoop, calls=%fused_computation.502 | loop fusion | bytes 3145728 | tf_op jit(solution)/shard_map/cos | solution.py:150
  54.9 4.8 %fusion.17 = (f32[512,512]{1,0:T(8,128)S(1)}, f32[512,512]{1,0:T(8,128)S(1)}) fusion(f32[1,512,512]{2,1,0:T(8,128)S(1)} %get-tuple-element.20, f32[1,512,512]{2,1,0:T(8,128)S(1)} %get-tuple-element.19, s32[512]{0:T(512)S(1)} %get-tuple-element.35, s32[512]{0:T(512)S(1)} %get-tuple-element.36), kind=kLoop, calls=%fused_computation.52 | loop fusion | flops 5242880 | bytes 4198400 | tf_op jit(solution)/shard_map/add | solution.py:33
  59.7 1.6 fusion.52
  61.3 1.6 fusion.50
  62.9 1.6 convolution_subtract_fusion.7
  64.5 1.8 multiply_add_fusion.3
  66.3 1.5 fusion.44
  67.9 1.5 fusion.46
  69.4 1.5 convolution_subtract_fusion.6
  71.5 2.0 reshape_reshape.6
  73.5 2.6 %copy.140 = f32[512,8,64]{0,1,2:T(8,128)S(1)} copy(f32[512,8,64]{2,1,0:T(8,128)} %reshape_reshape.6) | data formatting | bytes 2097152 | tf_op jit(solution)/shard_map/reshape;reshape | solution.py:84
  76.1 2.1 fusion.202
  78.1 2.0 fusion.208
  80.1 1.5 convolution_add_fusion.6
  82.7 1.2 copy.144
  83.9 2.4 %convolution_add_fusion.5 = f32[8,512,64]{1,0,2:T(8,128)S(1)} fusion(f32[8,512,64]{1,0,2:T(8,128)} %fusion.202, f32[512,8,64]{0,1,2:T(8,128)S(1)} %copy.144), kind=kOutput, calls=%fused_computation.27 | convolution fusion | flops 25428864 | bytes 3145728 | tf_op jit(solution)/shard_map/rmn,mj->rjn/dot_general | solution.py:26
  86.3 1.3 add_bitcast_fusion
  87.6 1.7 fusion.40
  89.3 2.2 fusion.38
  91.5 1.8 convolution_subtract_fusion.4
  93.3 1.8 convolution_add_fusion.4
  95.2 5.8 %fusion.87 = f32[512,8,64]{0,2,1:T(8,128)S(1)} fusion(f32[512,8,64]{0,2,1:T(8,128)S(1)} %convolution_add_fusion.4, f32[512,8,64]{0,2,1:T(8,128)S(1)} %convolution_subtract_fusion.4, s32[8,64]{1,0:T(8,128)S(1)} %fusion.199, s32[512]{0:T(512)S(1)} %fusion.239), kind=kOutput, calls=%fused_computation.149 | convolution fusion | flops 207151104 | bytes 3149824 | tf_op jit(solution)/shard_map/rjk,kn->rjn/dot_general | solution.py:25
  101.0 6.0 %fusion.93 = f32[512,8,64]{0,2,1:T(8,128)S(1)} fusion(f32[512,8,64]{0,2,1:T(8,128)S(1)} %convolution_add_fusion.4, f32[512,8,64]{0,2,1:T(8,128)S(1)} %convolution_subtract_fusion.4, s32[8,64]{1,0:T(8,128)S(1)} %fusion.199, s32[512]{0:T(512)S(1)} %fusion.239), kind=kOutput, calls=%fused_computation.155 | convolution fusion | flops 207151104 | bytes 3149824 | tf_op jit(solution)/shard_map/rjk,kn->rjn/dot_general | solution.py:23
  107.0 5.9 %convolution_subtract_fusion.3 = f32[512,8,64]{0,2,1:T(8,128)S(1)} fusion(f32[512,8,64]{0,2,1:T(8,128)S(1)} %fusion.93, f32[512,8,64]{0,2,1:T(8,128)S(1)} %convolution_add_fusion.4, f32[512,8,64]{0,2,1:T(8,128)S(1)} %convolution_subtract_fusion.4, s32[8,64]{1,0:T(8,128)S(1)} %fusion.199, s32[512]{0:T(512)S(1)} %fusion.239), kind=kOutput, calls=%fused_computation.24 | convolution fusion | flops 207413248 | bytes 4198400 | tf_op jit(solution)/shard_map/rjk,kn->rjn/dot_general | solution.py:24
  112.9 6.5 %multiply_add_fusion.1 = (f32[512,8,64]{0,2,1:T(8,128)S(1)}, f32[512,8,64]{0,2,1:T(8,128)S(1)}) fusion(f32[512,8,64]{0,2,1:T(8,128)S(1)} %convolution_subtract_fusion.3, f32[8,64]{1,0:T(8,128)S(1)} %get-tuple-element.39, f32[8,64]{1,0:T(8,128)S(1)} %get-tuple-element.40, f32[512,8,64]{0,2,1:T(8,128)S(1)} %fusion.87, ...), kind=kOutput, calls=%fused_computation.59 | convolution fusion | flops 208986112 | bytes 6299648 | tf_op jit(solution)/shard_map/rjk,kn->rjn/dot_general | solution.py:26
  119.4 1.5 fusion.32
  120.9 2.5 %fusion.34 = f32[8,512,64]{1,0,2:T(8,128)} fusion(f32[512,8,64]{0,2,1:T(8,128)S(1)} %get-tuple-element.14), kind=kOutput, calls=%fused_computation.85 | convolution fusion | flops 25166720 | bytes 2097152 | tf_op jit(solution)/shard_map/rjn,jm->rmn/dot_general | solution.py:23
  123.4 1.5 fusion.3
  126.6 3.3 %fusion.5 = f32[512,8,64]{0,1,2:T(8,128)S(1)} fusion(f32[8,512,64]{1,0,2:T(8,128)} %fusion.34, f32[512,8,64]{0,2,1:T(8,128)} %copy-done.1), kind=kOutput, calls=%fused_computation.22 | convolution fusion | flops 25691008 | bytes 3145728 | tf_op jit(solution)/shard_map/rjn,jm->rmn/dot_general | solution.py:24
  129.9 2.4 %copy.155 = f32[512,8,64]{2,1,0:T(8,128)} copy(f32[512,8,64]{0,1,2:T(8,128)S(1)} %fusion.5) | data formatting | bytes 2097152 | tf_op jit(solution)/shard_map/mul | solution.py:112
  132.2 1.9 mul.1101
  134.2 1.5 fusion.28
  135.7 1.5 fusion.26
  137.2 1.5 convolution_subtract_fusion.1
  138.8 1.7 multiply_add_fusion
  140.5 1.6 fusion.22
  142.1 1.6 fusion.1
  144.4 1.6 fusion.20
  146.0 1.8 fusion
  148.5 4.7 %cosine_bitcast_fusion = (f32[512,512]{1,0:T(8,128)S(1)}, f32[512,512]{1,0:T(8,128)S(1)}) fusion(f32[1,512,512]{2,1,0:T(8,128)} %all-gather.7.cloned.1.call-done), kind=kLoop, calls=%fused_computation.56 | loop fusion | bytes 3145728 | tf_op jit(solution)/shard_map/cos | solution.py:150
  158.9 1.3 pad_maximum_fusion
  160.2 3.9 %all-to-all-start = ((f32[2,1,512,128]{3,1,0,2:T(1,128)}), f32[2,1,512,128]{3,1,0,2:T(1,128)S(1)}, u32[]{:S(2)}, u32[]{:S(2)}) async-start(f32[2,1,512,128]{3,1,0,2:T(1,128)} %bitcast.44), calls=%async_computation | async-start | bytes 1048576 | tf_op jit(solution)/shard_map/all_to_all | solution.py:177
  165.4 13.1 %all-to-all-done = f32[2,1,512,128]{3,1,0,2:T(1,128)S(1)} async-done(((f32[2,1,512,128]{3,1,0,2:T(1,128)}), f32[2,1,512,128]{3,1,0,2:T(1,128)S(1)}, u32[]{:S(2)}, u32[]{:S(2)}) %all-to-all-start) | async-done | bytes 524320 | tf_op jit(solution)/shard_map/all_to_all | solution.py:177
  182.3 32.1 %psum.7 = f32[4,32]{1,0:T(4,128)S(1)} all-reduce(f32[4,32]{1,0:T(4,128)S(1)} %broadcast_select_fusion), channel_id=1, replica_groups=mesh['groups'=2,'beam'=16] {'beam'}, use_global_device_ids=true, to_apply=%region_1.2 | all-reduce | flops 128 | bytes 1024 | tf_op jit(solution)/shard_map/psum | solution.py:200
  (58 shorter events, 17.5 us)
Async XLA Ops:
  6.5 158.8 %copy-start = (s32[4,32,2]{1,2,0:T(2,128)S(1)}, s32[4,32,2]{1,2,0:T(2,128)}, u32[]{:S(2)}) copy-start(s32[4,32,2]{1,2,0:T(2,128)} %param.10) | copy-start | bytes 3076
  6.5 43.7 %all-gather.5.cloned.1.call-start = ((), (), s32[]{:S(2)}) async-start(), calls=%async_computation.1 | async-start | bytes 1114112 | tf_op jit(solution)/shard_map/all_gather | solution.py:149
  8.1 140.4 %all-gather.7.cloned.1.call-start = ((), (), s32[]{:S(2)}) async-start(), calls=%async_computation.2 | async-start | bytes 1114112 | tf_op jit(solution)/shard_map/all_gather | solution.py:149
  83.9 2.4 %copy-start.2 = (f32[8,512,64]{1,0,2:T(8,128)S(1)}, f32[8,512,64]{1,0,2:T(8,128)}, u32[]{:S(2)}) copy-start(f32[8,512,64]{1,0,2:T(8,128)} %fusion.208) | copy-start | bytes 3145732
  119.3 4.0 %copy-start.1 = (f32[512,8,64]{0,2,1:T(8,128)}, f32[512,8,64]{0,2,1:T(8,128)S(1)}, u32[]{:S(2)}) copy-start(f32[512,8,64]{0,2,1:T(8,128)S(1)} %get-tuple-element.13) | copy-start | bytes 3145732
  156.9 8.5 %copy-start.5 = (s32[16,2]{0,1:T(2,128)S(1)}, s32[16,2]{0,1:T(2,128)}, u32[]{:S(2)}) copy-start(s32[16,2]{0,1:T(2,128)} %param.7) | copy-start | bytes 388
  158.2 20.6 %copy-start.3 = (f32[16]{0:T(128)S(1)}, f32[16]{0:T(128)}, u32[]{:S(2)}) copy-start(f32[16]{0:T(128)} %param.8) | copy-start | bytes 196
  158.2 20.6 %copy-start.4 = (f32[16]{0:T(128)S(1)}, f32[16]{0:T(128)}, u32[]{:S(2)}) copy-start(f32[16]{0:T(128)} %param.9) | copy-start | bytes 196
  160.2 18.3 %all-to-all-start = ((f32[2,1,512,128]{3,1,0,2:T(1,128)}), f32[2,1,512,128]{3,1,0,2:T(1,128)S(1)}, u32[]{:S(2)}, u32[]{:S(2)}) async-start(f32[2,1,512,128]{3,1,0,2:T(1,128)} %bitcast.44), calls=%async_computation | async-start | bytes 1048576 | tf_op jit(solution)/shard_map/all_to_all | solution.py:177
Sparse Core Ops, SparseCore 0:
  9.5 40.6 all-gather.4
  52.4 36.8 all-gather.6
where the time goes:
time: 226 us; the launch traced here: 222 us
  matrix products  82.3 us (36%)
  waiting for transfers between devices  47 us (21%)
  blocking collectives  32.1 us (14%)
  local copies, waits for them, and re-layouts  28.8 us (13%)
  between operations  19.3 us (9%)
  other arithmetic  9.01 us (4%)
  starting transfers between devices  3.93 us (2%)
    all_gather x2, waiting for transfers between devices, per_device(): lax.all_gather(potential[layer_index], 'beam', axis=0, tiled=True)  33.3 us
    psum x1, blocking collectives, per_device(): totals = lax.psum(tile_slots, 'beam')  32.1 us
    dot_general x11, matrix products, complex_einsum(): imag_real = jnp.einsum(formula, left_imag, right_real, precision=precise)  21.2 us
    dot_general x11, matrix products, complex_einsum(): imag_imag = jnp.einsum(formula, left_imag, right_imag, precision=precise)  20.8 us
    dot_general x11, matrix products, complex_einsum(): real_real = jnp.einsum(formula, left_real, right_real, precision=precise)  20.5 us
    dot_general x11, matrix products, complex_einsum(): real_imag = jnp.einsum(formula, left_real, right_imag, precision=precise)  19.8 us
    all_to_all x1, waiting for transfers between devices, per_device(): lax.all_to_all(payload, 'beam', split_axis=2, concat_axis=1, tiled=True)  13.1 us
    cos x2, local copies, waits for them, and re-layouts, per_device(): trans_real = jnp.cos(full_slice)  9.32 us
  transfers between devices with their start and end apart: 3, of which 2 were waited for; matrix products, arithmetic and copies ran while one was open for 46% of the time, Pallas kernels for 0%

commit v1 on v0

v1 whole, which is shorter than its diff:
```python
import functools

import jax
import jax.numpy as jnp
import numpy as np
from jax import lax
from jax.experimental import pallas as pl
from jax.experimental.pallas import tpu as pltpu
from jax.sharding import PartitionSpec as P

CROP = 256
TILE = 128
MAX_TILT = 16
F32 = jnp.float32
BF16 = jnp.bfloat16
MESH = pl.DeviceIdType.MESH
LIMIT = 56 * 1024 * 1024


def split(value):
    high = value.astype(BF16)
    return high, (value - high.astype(F32)).astype(BF16)


def np_split(value):
    value = value.astype(np.float32)
    high = value.astype(BF16)
    return high, (value - high.astype(np.float32)).astype(BF16)


def mm(left, right):
    return jnp.dot(left, right, preferred_element_type=F32)


def polys(r):
    s = r * r
    sin = r + r * s * (-1.0 / 6 + s * (1.0 / 120 + s * (-1.0 / 5040 + s * (1.0 / 362880))))
    cos = 1.0 + s * (-0.5 + s * (1.0 / 24 + s * (-1.0 / 720 + s * (1.0 / 40320))))
    return cos, sin


def cos_sin(x):
    q = jnp.floor(x * (2.0 / np.pi) + 0.5)
    r = (x - q * 1.5703125) - q * 4.838267948966e-4
    cos, sin = polys(r)
    half = q * 0.5
    whole = jnp.floor(half)
    odd = half != whole
    c = jnp.where(odd, sin, cos)
    s = jnp.where(odd, cos, sin)
    quarter = jnp.floor(half * 0.5)
    upper = (whole - 2.0 * quarter) > 0.5
    flip_c = odd != upper
    return jnp.where(flip_c, -c, c), jnp.where(upper, -s, s)


def cos_sin_int(m, period):
    m = m & (period - 1)
    quarter = period // 4
    q = lax.shift_right_logical(
        m + quarter // 2, int(np.log2(quarter))
    )
    r = (m - q * quarter).astype(F32) * (2.0 * np.pi / period)
    cos, sin = polys(r)
    odd = (q & 1) == 1
    c = jnp.where(odd, sin, cos)
    s = jnp.where(odd, cos, sin)
    return jnp.where(((q + 1) & 2) == 2, -c, c), jnp.where((q & 2) == 2, -s, s)


def half_band(length):
    reach = int(np.sqrt((length * length - 1) // 9)) + MAX_TILT
    return -(-(reach + 1) // 64) * 64


def forward_tables(length):
    half = half_band(length)
    grid = np.arange(length)
    k = np.arange(-half, half)
    angle = 2 * np.pi / length * ((grid[:, None] * k[None, :]) % length)
    c, s = np.cos(angle), np.sin(angle)
    cols = np.concatenate(
        (np.concatenate((c, -s), 1), np.concatenate((s, c), 1)), 0
    )
    k = np.arange(half)
    angle = 2 * np.pi / length * ((k[:, None] * grid[None, :]) % length)
    rows = np.concatenate((np.cos(angle), np.sin(angle)), 0)
    return np_split(cols) + np_split(rows)


def forward_kernel(
    n, remote, own_ref, crop_ref, ch_any, cl_any, rh_any, rl_any, qh_ref, ql_ref, *rest
):
    if remote:
        t1_ref, buf, buf1, ch, cl, rh, rl, th, tl, uh, ul, tab_sem, s0, r0, s1, r1 = rest
    else:
        ch, cl, rh, rl, th, tl, uh, ul, tab_sem = rest
    pairs = ((ch_any, ch), (cl_any, cl), (rh_any, rh), (rl_any, rl))
    tables = [
        pltpu.make_async_copy(src, dst, tab_sem.at[i]) for i, (src, dst) in enumerate(pairs)
    ]
    for copy in tables:
        copy.start()
    length = th.shape[0]
    half = rh.shape[0] // 2
    band = 2 * half

    def transmit(value, row, count):
        c, s = cos_sin(value)
        h, l = split(c)
        th[pl.ds(row, count), :length] = h
        tl[pl.ds(row, count), :length] = l
        h, l = split(s)
        th[pl.ds(row, count), length:] = h
        tl[pl.ds(row, count), length:] = l

    if remote:
        rows = own_ref.shape[0]
        groups = lax.axis_index("groups")
        me = lax.axis_index("beam")
        planes = n // 4
        plane, low = me // 4, me % 4
        across = plane * 4 + (low + 2) % 4
        sibling = plane * 4 + (low // 2) * 2 + (1 - low % 2)

        def peer(step):
            return ((plane + step) % planes) * 4 + low

        barrier = pltpu.get_barrier_semaphore()
        friends = [across, sibling] + [peer(step) for step in range(1, planes)]
        for friend in friends:
            pl.semaphore_signal(barrier, inc=1, device_id=(groups, friend), device_id_type=MESH)
        pl.semaphore_wait(barrier, len(friends))

        def push(which, src, block, target, send_index):
            dst, ss, rs = ((buf, s0, r0), (buf1, s1, r1))[which]
            return pltpu.make_async_remote_copy(
                src_ref=src,
                dst_ref=dst.at[block],
                send_sem=ss.at[send_index],
                recv_sem=rs.at[block],
                device_id=(groups, target),
                device_id_type=MESH,
            )

        started = []

        def go(which, src, block, target, index):
            copy = push(which, src, block, target, index)
            copy.start()
            started.append(copy)

        def arrive(which, block):
            src = (own_ref, crop_ref)[which]
            push(which, src, block, sibling, 0).wait_recv()

        order = [1, planes - 1] + [s for s in range(2, planes - 1)]
        order = [s for i, s in enumerate(order) if s not in order[:i]]

        def open_round(which):
            src = (own_ref, crop_ref)[which]
            go(which, src, me, across, 0)
            for i, step in enumerate(order):
                go(which, src, me, peer(step), 1 + i)
            go(which, src, me, sibling, planes)

        def forward_round(which, work):
            dst = (buf, buf1)[which]
            index = planes + 1
            work(me, (own_ref, crop_ref)[which])
            for step in [0] + order:
                base = ((plane + step) % planes) * 4
                if step != 0:
                    block = base + low
                    arrive(which, block)
                    go(which, dst.at[block], block, across, index)
                    go(which, dst.at[block], block, sibling, index + 1)
                    index += 2
                    work(block, dst.at[block])
                block = base + (low + 2) % 4
                arrive(which, block)
                go(which, dst.at[block], block, sibling, index)
                index += 1
                work(block, dst.at[block])
            for step in [0] + order:
                base = ((plane + step) % planes) * 4
                for block in (
                    base + (low // 2) * 2 + (1 - low % 2),
                    base + (1 - low // 2) * 2 + (1 - low % 2),
                ):
                    arrive(which, block)
                    work(block, dst.at[block])

        def work0(block, ref):
            transmit(ref[...], pl.multiple_of(block * rows, rows), rows)

        def work1(block, ref):
            t1_ref[pl.ds(pl.multiple_of(block * rows, rows), rows), :] = ref[...]

        open_round(0)
        forward_round(0, work0)
        open_round(1)
    else:
        transmit(own_ref[...], 0, length)

    for copy in tables:
        copy.wait()

    step_rows = 256

    def stage_one(i, carry):
        at = pl.multiple_of(i * step_rows, step_rows)
        h = th[pl.ds(at, step_rows), :]
        l = tl[pl.ds(at, step_rows), :]
        u = mm(h, ch[...]) + mm(l, ch[...]) + mm(h, cl[...])
        high, lower = split(u)
        uh[pl.ds(at, step_rows), :] = high
        ul[pl.ds(at, step_rows), :] = lower
        return carry

    lax.fori_loop(0, length // step_rows, stage_one, 0)
    if remote:
        forward_round(1, work1)
    for j in range(band // 128):
        a, b = slice(j * 128, j * 128 + 128), slice(band + j * 128, band + j * 128 + 128)
        h = jnp.concatenate((uh[:, a], uh[:, b]), 1)
        l = jnp.concatenate((ul[:, a], ul[:, b]), 1)
        p = mm(rh[...], h) + mm(rh[...], l) + mm(rl[...], h)
        cr, ci, sr, si = p[:half, :128], p[:half, 128:], p[half:, :128], p[half:, 128:]
        for at, real, imag in ((0, cr + si, ci - sr), (half, cr - si, ci + sr)):
            h, l = split(real)
            qh_ref[at : at + half, a] = h
            ql_ref[at : at + half, a] = l
            h, l = split(imag)
            qh_ref[at : at + half, b] = h
            ql_ref[at : at + half, b] = l
    if remote:
        for copy in started:
            copy.wait_send()


def forward(own, crop, n, length):
    rows = own.shape[0]
    half = half_band(length)
    band = 2 * half
    remote = rows % 16 == 0 and n % 4 == 0 and n > 4
    tables = [jnp.asarray(t) for t in forward_tables(length)]
    vmem = pl.BlockSpec(memory_space=pltpu.VMEM)
    scratch = [
        pltpu.VMEM((2 * length, 2 * band), BF16),
        pltpu.VMEM((2 * length, 2 * band), BF16),
        pltpu.VMEM((band, length), BF16),
        pltpu.VMEM((band, length), BF16),
        pltpu.VMEM((length, 2 * length), BF16),
        pltpu.VMEM((length, 2 * length), BF16),
        pltpu.VMEM((length, 2 * band), BF16),
        pltpu.VMEM((length, 2 * band), BF16),
        pltpu.SemaphoreType.DMA((4,)),
    ]
    outs = [jax.ShapeDtypeStruct((band, 2 * band), BF16)] * 2
    if remote:
        outs = outs + [jax.ShapeDtypeStruct((length, CROP), F32)]
        scratch = (
            [pltpu.VMEM((n, rows, length), F32), pltpu.VMEM((n, rows, CROP), F32)]
            + scratch
            + [pltpu.SemaphoreType.DMA((n,))] * 4
        )
        params = pltpu.CompilerParams(
            collective_id=0, has_side_effects=True, vmem_limit_bytes=LIMIT
        )
    else:
        own = lax.all_gather(own, "beam", axis=0, tiled=True)
        params = pltpu.CompilerParams(vmem_limit_bytes=LIMIT)
    result = pl.pallas_call(
        functools.partial(forward_kernel, n, remote),
        out_shape=outs,
        in_specs=[vmem, vmem] + [pl.BlockSpec(memory_space=pl.ANY)] * 4,
        out_specs=[vmem] * len(outs),
        scratch_shapes=scratch,
        compiler_params=params,
        name="forward",
    )(own, crop, *tables)
    if remote:
        return result
    return (*result, lax.all_gather(crop, "beam", axis=0, tiled=True))


def tile_tables():
    k = np.arange(TILE)
    angle = 2 * np.pi / TILE * ((k[:, None] * k[None, :]) % TILE)
    c, s = np.cos(angle), np.sin(angle)
    cols = np.concatenate((np.concatenate((c, -s), 1), np.concatenate((s, c), 1)), 0)
    rh, rl = np_split(np.concatenate((c, -s), 0))
    return np_split(cols) + (np.concatenate((rh, rh, rl), 1),)


def beam_kernel(
    length, beams, info, tilts, qh_ref, ql_ref, t1_ref, dh, dl, drow, spots, weights,
    out_ref, tr, ti, gcat, sr, si,
):
    beam = pl.program_id(0)
    band = qh_ref.shape[0]
    half = band // 2
    row0, col0, ky0 = info[0], info[1], info[2]
    ty, tx = tilts[2 * beam], tilts[2 * beam + 1]
    period = 2 * length

    @pl.when(beam == 0)
    def _():
        c, s = cos_sin(t1_ref[...])
        tr[...] = c
        ti[...] = s

    f = lax.broadcasted_iota(jnp.int32, (band, TILE), 0) - half + tx
    cell = lax.broadcasted_iota(jnp.int32, (band, TILE), 1) + col0
    c, s = cos_sin_int(f * (2 * cell - f), period)
    chi, clo = split(c)
    shi, slo = split(s)
    xh = jnp.concatenate(
        (jnp.concatenate((chi, shi), 1), jnp.concatenate((-shi, chi), 1)), 0
    )
    xl = jnp.concatenate(
        (jnp.concatenate((clo, slo), 1), jnp.concatenate((-slo, clo), 1)), 0
    )
    k = lax.broadcasted_iota(jnp.int32, (TILE, band), 1)
    f = jnp.where(k < half, k, half - k) + ty
    cell = lax.broadcasted_iota(jnp.int32, (TILE, band), 0) + row0
    c, s = cos_sin_int(f * (2 * cell - f), period)
    c = jnp.where(k == half, 0.0, c)
    s = jnp.where(k == half, 0.0, s)
    chi, clo = split(c)
    shi, slo = split(s)
    yh = jnp.concatenate((chi, shi), 0)
    yl = jnp.concatenate((clo, slo), 0)

    fx = (lax.broadcasted_iota(jnp.int32, (1, band), 1) - half + tx).astype(F32)
    fx2 = 9.0 * fx * fx
    chunk = 128
    for i in range(band // chunk):
        at = slice(i * chunk, i * chunk + chunk)
        k = lax.broadcasted_iota(jnp.int32, (chunk, 1), 0) + i * chunk
        fy = (jnp.where(k < half, k, half - k) + ty).astype(F32)
        keep = jnp.where(9.0 * fy * fy + fx2 < float(length * length), 1.0, 0.0).astype(BF16)
        keep = jnp.concatenate((keep, keep), 1)
        h = qh_ref[at, :] * keep
        l = ql_ref[at, :] * keep
        g = mm(h, xh) + mm(l, xh) + mm(h, xl)
        gh, gl = split(g)
        gcat[i * chunk : i * chunk + chunk, :] = gh
        gcat[band + i * chunk : band + i * chunk + chunk, :] = gl
        gcat[2 * band + i * chunk : 2 * band + i * chunk + chunk, :] = gh
    p = mm(jnp.concatenate((yh, yh, yl), 1), gcat[...])
    wr = p[:TILE, :TILE] - p[TILE:, TILE:]
    wi = p[:TILE, TILE:] + p[TILE:, :TILE]
    a, b = tr[...], ti[...]
    w = jnp.concatenate((wr * a - wi * b, wr * b + wi * a), 1)
    h, l = split(w)
    v = mm(h, dh[...]) + mm(l, dh[...]) + mm(h, dl[...])
    h, l = split(v)
    z = mm(drow[...], jnp.concatenate((h, l, h), 0))
    sr[pl.ds(beam, TILE, stride=beams), :] = z[:TILE, :TILE] - z[TILE:, TILE:]
    si[pl.ds(beam, TILE, stride=beams), :] = z[:TILE, TILE:] + z[TILE:, :TILE]

    @pl.when(beam == beams - 1)
    def _():
        probes = spots.shape[0]
        q = (spots[:, 0:1] + row0) * 1
        r = (spots[:, 1:2] + col0) * 1
        phase = weights[0:1, :].astype(jnp.int32) * q + weights[1:2, :].astype(jnp.int32) * r
        phase = (phase & (length - 1)).astype(F32)
        c, s = cos_sin(weights[3:4, :] - phase * (2.0 * np.pi / length))
        amp = weights[2:3, :] * (1.0 / (length * length))
        full = jnp.concatenate((c * amp, s * amp), 0)
        h = full.astype(BF16).astype(F32)
        lane = lax.broadcasted_iota(jnp.int32, full.shape, 1)
        coef = jnp.where(lane < 2 * beams, h, full - h).astype(BF16)

        def one(ky):
            at = pl.multiple_of(ky * beams, beams)
            both = jnp.concatenate((sr[pl.ds(at, beams), :], si[pl.ds(at, beams), :]), 1)
            h, l = split(both)
            e = mm(coef, jnp.concatenate((h, l, h), 0))
            er = e[:probes, :TILE] - e[probes:, TILE:]
            ei = e[:probes, TILE:] + e[probes:, :TILE]
            return er * er + ei * ei

        own = out_ref.shape[0]

        def mine(j, total):
            value = one(ky0 + j)
            out_ref[j] = value
            return total + value

        def others(j, total):
            return total + one((ky0 + own + j) & (TILE - 1))

        total = lax.fori_loop(0, own, mine, jnp.zeros((probes, TILE), F32), unroll=4)
        total = lax.fori_loop(0, TILE - own, others, total, unroll=4)
        level = jnp.sum(total, axis=1, keepdims=True) * (1.0 / (TILE * TILE))
        scale = 1.0 / (level + 1e-06)

        def norm(j, carry):
            out_ref[j] = out_ref[j] * scale
            return carry

        lax.fori_loop(0, own, norm, 0, unroll=4)


def per_device(potential, beam_tilts, aperture, aberration, probe_spots, crop_anchor, n):
    length = potential.shape[2]
    beams = beam_tilts.shape[0]
    per_side = CROP // TILE
    device = lax.axis_index("beam")
    crop_rows = lax.dynamic_slice(potential[1], (0, crop_anchor[1]), (potential.shape[1], CROP))
    qh, ql, t1 = forward(potential[0], crop_rows, n, length)
    own = per_side * per_side * TILE // n
    my_tile = device * own // TILE
    row0 = crop_anchor[0] + TILE * (my_tile // per_side)
    col_at = TILE * (my_tile % per_side)
    col0 = crop_anchor[1] + col_at
    t1 = lax.dynamic_slice(t1, (row0, col_at), (TILE, TILE))
    spots = lax.dynamic_slice_in_dim(probe_spots, my_tile, 1, 0)[0]
    info = jnp.stack((row0, col0, device * own % TILE))
    weights = jnp.concatenate(
        (beam_tilts.T.astype(F32), aperture[None], aberration[None]), 0
    )
    weights = jnp.concatenate((weights,) * 3, 1)
    dh, dl, drow = [jnp.asarray(t) for t in tile_tables()]
    probes = spots.shape[0]
    smem = pl.BlockSpec(memory_space=pltpu.SMEM)
    vmem = pl.BlockSpec(memory_space=pltpu.VMEM)
    return pl.pallas_call(
        functools.partial(beam_kernel, length, beams),
        grid=(beams,),
        out_shape=jax.ShapeDtypeStruct((own, probes, TILE), F32),
        in_specs=[smem, smem] + [vmem] * 8,
        out_specs=vmem,
        scratch_shapes=[
            pltpu.VMEM((TILE, TILE), F32),
            pltpu.VMEM((TILE, TILE), F32),
            pltpu.VMEM((3 * qh.shape[0], 2 * TILE), BF16),
            pltpu.VMEM((TILE * beams, TILE), F32),
            pltpu.VMEM((TILE * beams, TILE), F32),
        ],
        compiler_params=pltpu.CompilerParams(vmem_limit_bytes=LIMIT),
        name="beams",
    )(info, beam_tilts.reshape(-1), qh, ql, t1, dh, dl, drow, spots, weights)


def solution(mesh):
    placed = (P("groups", "beam", None), P(), P(), P(), P("groups", None, None), P("groups"))
    return jax.shard_map(
        functools.partial(per_device, n=mesh.shape["beam"]),
        mesh=mesh,
        in_specs=placed,
        out_specs=P(("groups", "beam"), None, None),
        check_vma=False,
    )
```

time: 226 us -> 91.5 us (0.40)
  matrix products: 82.3 us -> 0 us
  Pallas kernels: 0 us -> 78 us
  waiting for transfers between devices: 47 us -> 0 us
  blocking collectives: 32.1 us -> 0 us
  local copies, waits for them, and re-layouts: 28.8 us -> 7.33 us
  between operations: 19.3 us -> 3.5 us
  other arithmetic: 9.01 us -> 1.3 us
  starting transfers between devices: 3.93 us -> 0 us
    dot_general x44 -> x0, matrix products: 82.3 us -> none  [the longest x11 21.2 us: complex_einsum(): imag_real = jnp.einsum(formula, left_imag, right_real, precision=precise)]
    pallas_call x0 -> x2, Pallas kernels: none -> 78 us  [the longest x1 41.1 us: per_device(): pl.pallas_call(functools.partial(beam_kernel, length, beams), grid=(beams...]
    all_gather x2 -> x0, waiting for transfers between devices: 33.3 us -> none  [per_device(): lax.all_gather(potential[layer_index], 'beam', axis=0, tiled=True)]
    psum x1 -> x0, blocking collectives: 32.1 us -> none  [per_device(): totals = lax.psum(tile_slots, 'beam')]
    all_to_all x1 -> x0, waiting for transfers between devices: 13.1 us -> none  [per_device(): lax.all_to_all(payload, 'beam', split_axis=2, concat_axis=1, tiled=True)]
    cos x3 -> x0, local copies, waits for them, and re-layouts: 9.4 us -> none  [the longest x2 9.32 us: per_device(): trans_real = jnp.cos(full_slice)]
    mul x8 -> x0, local copies, waits for them, and re-layouts: 7.23 us -> none  [the longest x2 4.28 us: cols_inverse(): done_real.reshape(height, length) * inverse_scale]
    another operation x4 -> x0, local copies, waits for them, and re-layouts: 6.13 us -> none  [the longest x2 4.54 us: cols_forward(): blocks_real = field_real.reshape(height, 8, inner_size)]
  transfers between devices with their start and end apart: 3 -> 0, of which waited for: 2 -> 0; matrix products, arithmetic and copies ran while one was open for 46% -> 0% of each run, Pallas kernels for 0% -> 0%
where the time goes in v1:
time: 91.5 us; the launch traced here: 90.1 us
  Pallas kernels  78 us (85%)
  local copies, waits for them, and re-layouts  7.33 us (8%)
  between operations  3.5 us (4%)
  other arithmetic  1.3 us (1%)
    pallas_call x1, Pallas kernels, per_device(): pl.pallas_call(functools.partial(beam_kernel, length, beams), grid=(beams...  41.1 us
    pallas_call x1, Pallas kernels, forward(): pl.pallas_call(functools.partial(forward_kernel, n, remote), out_shape=ou...  37 us

profile of v1, /device:TPU:0, one launch (start us, length us, event | category | flops | bytes accessed | tf_op | source)
XLA Modules:
  0.0 90.1 jit_solution(15316407888336715602)
XLA Ops:
  0.0 0.0 copy-start
  0.0 1.4 %fusion.1 = (s32[1]{0:T(128)}, s32[1]{0:T(128)}) fusion(s32[2]{0:T(128)} %param.18), kind=kLoop, calls=%fused_computation.7 | loop fusion | bytes 16 | tf_op jit(solution)/shard_map/slice | solution.py:418
  2.8 0.6 pad_add_fusion.info
  3.4 0.8 copy.16
  4.2 0.7 reshape.4.tilts
  4.9 1.5 %fusion = (f32[1,32,512]{2,1,0:T(8,128)S(1)}, f32[32,512]{1,0:T(8,128)}) fusion(f32[2,32,512]{2,1,0:T(8,128)} %param.13), kind=kLoop, calls=%fused_computation.6 | loop fusion | bytes 262144 | tf_op jit(solution)/shard_map/slice | solution.py:414
  8.4 0.7 dynamic-slice_bitcast_fusion.crop_ref
  9.1 0.0 copy-start.1
  9.1 0.0 copy-start.2
  9.1 0.0 copy-start.3
  9.1 37.0 %forward.1 = (bf16[384,768]{1,0:T(8,128)(2,1)}, bf16[384,768]{1,0:T(8,128)(2,1)}, f32[512,256]{1,0:T(8,128)}) custom-call(f32[32,512]{1,0:T(8,128)} %get-tuple-element.12.own_ref, f32[32,256]{1,0:T(8,128)} %dynamic-slice_bitcast_fusion.crop_ref, bf16[1024,768]{1,0:T(8,128)(2,1)} %constant.71.clone.ch_any, bf16[1024,768]{1,0:T(8,128)(2,1)} %constant.72.clone.cl_any, ...), custom_call_target="tpu_custom_call" | custom-call | tf_op jit(solution)/shard_map/forward/pallas_call | solution.py:274
  46.1 1.6 %dynamic_slice.13.t1_ref = f32[128,128]{1,0:T(8,128)} dynamic-slice(f32[512,256]{1,0:T(8,128)} %get-tuple-element.10, s32[]{:T(128)S(6)} %select_n.35, s32[]{:T(128)S(6)} %select_n.36), dynamic_slice_sizes={128,128} | dynamic-slice | bytes 131076 | tf_op jit(solution)/shard_map/dynamic_slice | solution.py:421
  47.7 0.0 copy-done
  47.7 0.7 copy.17.spots
  48.4 0.0 copy-done.1
  48.4 0.0 copy-done.2
  48.4 0.0 copy-done.3
  48.4 0.7 maximum_maximum_fusion.weights
  49.1 41.1 %beams.1 = f32[32,32,128]{2,1,0:T(8,128)} custom-call(s32[3]{0:T(128)} %pad_add_fusion.info, s32[32]{0:T(128)} %reshape.4.tilts, bf16[384,768]{1,0:T(8,128)(2,1)} %get-tuple-element.8.qh_ref, bf16[384,768]{1,0:T(8,128)(2,1)} %get-tuple-element.9.ql_ref, f32[128,128]{1,0:T(8,128)} %dynamic_slice.13.t1_ref, bf16[256,256]{1,0:T(8,128)(2,1)} %constant.75.clone.dh, ...), custom_call_target="tpu_custom_call" | custom-call | tf_op jit(solution)/shard_map/beams/pallas_call | solution.py:432
  (2 shorter events, 0.0 us)
Async XLA Ops:
  0.0 47.7 %copy-start = (s32[4,32,2]{1,2,0:T(2,128)S(1)}, s32[4,32,2]{1,2,0:T(2,128)}, u32[]{:S(2)}) copy-start(s32[4,32,2]{1,2,0:T(2,128)} %param.17) | copy-start | bytes 3076
  9.1 39.3 %copy-start.1 = (s32[16,2]{0,1:T(2,128)S(1)}, s32[16,2]{0,1:T(2,128)}, u32[]{:S(2)}) copy-start(s32[16,2]{0,1:T(2,128)} %param.14) | copy-start | bytes 388
  9.1 39.3 %copy-start.2 = (f32[16]{0:T(128)S(1)}, f32[16]{0:T(128)}, u32[]{:S(2)}) copy-start(f32[16]{0:T(128)} %param.16) | copy-start | bytes 196
  9.1 39.3 %copy-start.3 = (f32[16]{0:T(128)S(1)}, f32[16]{0:T(128)}, u32[]{:S(2)}) copy-start(f32[16]{0:T(128)} %param.15) | copy-start | bytes 196

commit v2 on v1

--- a/solution.py
+++ b/solution.py
@@ -143,6 +143,9 @@
                 device_id_type=MESH,
             )
 
+        def own_part(which, target):
+            return own_ref if which == 0 else crop_ref.at[(target // 4) % (CROP // TILE)]
+
         started = []
 
         def go(which, src, block, target, index):
@@ -151,23 +154,21 @@
             started.append(copy)
 
         def arrive(which, block):
-            src = (own_ref, crop_ref)[which]
-            push(which, src, block, sibling, 0).wait_recv()
+            push(which, own_part(which, me), block, sibling, 0).wait_recv()
 
         order = [1, planes - 1] + [s for s in range(2, planes - 1)]
         order = [s for i, s in enumerate(order) if s not in order[:i]]
 
         def open_round(which):
-            src = (own_ref, crop_ref)[which]
-            go(which, src, me, across, 0)
+            go(which, own_part(which, me), me, across, 0)
             for i, step in enumerate(order):
-                go(which, src, me, peer(step), 1 + i)
-            go(which, src, me, sibling, planes)
+                go(which, own_part(which, peer(step)), me, peer(step), 1 + i)
+            go(which, own_part(which, me), me, sibling, planes)
 
         def forward_round(which, work):
             dst = (buf, buf1)[which]
             index = planes + 1
-            work(me, (own_ref, crop_ref)[which])
+            work(me, own_part(which, me))
             for step in [0] + order:
                 base = ((plane + step) % planes) * 4
                 if step != 0:
@@ -198,8 +199,8 @@
             t1_ref[pl.ds(pl.multiple_of(block * rows, rows), rows), :] = ref[...]
 
         open_round(0)
+        open_round(1)
         forward_round(0, work0)
-        open_round(1)
     else:
         transmit(own_ref[...], 0, length)
 
@@ -243,7 +244,7 @@
     rows = own.shape[0]
     half = half_band(length)
     band = 2 * half
-    remote = rows % 16 == 0 and n % 4 == 0 and n > 4
+    remote = rows % 16 == 0 and n == 4 * (CROP // TILE) ** 2
     tables = [jnp.asarray(t) for t in forward_tables(length)]
     vmem = pl.BlockSpec(memory_space=pltpu.VMEM)
     scratch = [
@@ -259,9 +260,9 @@
     ]
     outs = [jax.ShapeDtypeStruct((band, 2 * band), BF16)] * 2
     if remote:
-        outs = outs + [jax.ShapeDtypeStruct((length, CROP), F32)]
+        outs = outs + [jax.ShapeDtypeStruct((length, TILE), F32)]
         scratch = (
-            [pltpu.VMEM((n, rows, length), F32), pltpu.VMEM((n, rows, CROP), F32)]
+            [pltpu.VMEM((n, rows, length), F32), pltpu.VMEM((n, rows, TILE), F32)]
             + scratch
             + [pltpu.SemaphoreType.DMA((n,))] * 4
         )
@@ -282,7 +283,11 @@
     )(own, crop, *tables)
     if remote:
         return result
-    return (*result, lax.all_gather(crop, "beam", axis=0, tiled=True))
+    tile = lax.axis_index("beam") * (CROP // TILE) ** 2 // n
+    crop = lax.dynamic_index_in_dim(
+        lax.all_gather(crop, "beam", axis=1, tiled=True), tile % (CROP // TILE), 0, False
+    )
+    return (*result, crop)
 
 
 def tile_tables():
@@ -295,19 +300,44 @@
 
 
 def beam_kernel(
-    length, beams, info, tilts, qh_ref, ql_ref, t1_ref, dh, dl, drow, spots, weights,
-    out_ref, tr, ti, gcat, sr, si,
+    length, beams, n, tilts, anchor, qh_ref, ql_ref, t1_ref, dh, dl, drow, spots_ref, weights,
+    out_ref, tr, ti, gcat, sr, si, sent, got, send_sem, recv_sem,
 ):
-    beam = pl.program_id(0)
+    step = pl.program_id(0)
+    steps = beams // 2
+    groups = lax.axis_index("groups")
+    me = lax.axis_index("beam")
+    core = me % 2
+    sibling = me + 1 - 2 * core
+    beam = core * steps + step
+    own = out_ref.shape[0]
+    per_side = CROP // TILE
+    my_tile = me * own // TILE
+    ky0 = me * own % TILE
+    col_at = pl.multiple_of((my_tile % per_side) * TILE, TILE)
+    row0 = anchor[0] + TILE * (my_tile // per_side)
+    col0 = anchor[1] + col_at
     band = qh_ref.shape[0]
     half = band // 2
-    row0, col0, ky0 = info[0], info[1], info[2]
-    ty, tx = tilts[2 * beam], tilts[2 * beam + 1]
+    ty, tx = tilts[beam, 0], tilts[beam, 1]
     period = 2 * length
 
-    @pl.when(beam == 0)
+    def share(at):
+        return pltpu.make_async_remote_copy(
+            src_ref=sent.at[at],
+            dst_ref=got.at[at],
+            send_sem=send_sem.at[at],
+            recv_sem=recv_sem.at[at],
+            device_id=(groups, sibling),
+            device_id_type=MESH,
+        )
+
+    @pl.when(step == 0)
     def _():
-        c, s = cos_sin(t1_ref[...])
+        barrier = pltpu.get_barrier_semaphore()
+        pl.semaphore_signal(barrier, inc=1, device_id=(groups, sibling), device_id_type=MESH)
+        pl.semaphore_wait(barrier, 1)
+        c, s = cos_sin(t1_ref[pl.ds(row0, TILE), :])
         tr[...] = c
         ti[...] = s
 
@@ -335,20 +365,18 @@
 
     fx = (lax.broadcasted_iota(jnp.int32, (1, band), 1) - half + tx).astype(F32)
     fx2 = 9.0 * fx * fx
-    chunk = 128
-    for i in range(band // chunk):
-        at = slice(i * chunk, i * chunk + chunk)
-        k = lax.broadcasted_iota(jnp.int32, (chunk, 1), 0) + i * chunk
-        fy = (jnp.where(k < half, k, half - k) + ty).astype(F32)
-        keep = jnp.where(9.0 * fy * fy + fx2 < float(length * length), 1.0, 0.0).astype(BF16)
-        keep = jnp.concatenate((keep, keep), 1)
-        h = qh_ref[at, :] * keep
-        l = ql_ref[at, :] * keep
-        g = mm(h, xh) + mm(l, xh) + mm(h, xl)
-        gh, gl = split(g)
-        gcat[i * chunk : i * chunk + chunk, :] = gh
-        gcat[band + i * chunk : band + i * chunk + chunk, :] = gl
-        gcat[2 * band + i * chunk : 2 * band + i * chunk + chunk, :] = gh
+    k = lax.broadcasted_iota(jnp.int32, (band, 1), 0)
+    fy = (jnp.where(k < half, k, half - k) + ty).astype(F32)
+    keep = jnp.where(9.0 * fy * fy + fx2 < float(length * length), 1.0, 0.0).astype(BF16)
+    keep = jnp.concatenate((keep, keep), 1)
+    h = qh_ref[...] * keep
+    l = ql_ref[...] * keep
+    both = mm(jnp.concatenate((h, l), 0), xh)
+    g = both[:band] + both[band:] + mm(h, xl)
+    gh, gl = split(g)
+    gcat[:band, :] = gh
+    gcat[band : 2 * band, :] = gl
+    gcat[2 * band :, :] = gh
     p = mm(jnp.concatenate((yh, yh, yl), 1), gcat[...])
     wr = p[:TILE, :TILE] - p[TILE:, TILE:]
     wi = p[:TILE, TILE:] + p[TILE:, :TILE]
@@ -358,11 +386,26 @@
     v = mm(h, dh[...]) + mm(l, dh[...]) + mm(h, dl[...])
     h, l = split(v)
     z = mm(drow[...], jnp.concatenate((h, l, h), 0))
-    sr[pl.ds(beam, TILE, stride=beams), :] = z[:TILE, :TILE] - z[TILE:, TILE:]
-    si[pl.ds(beam, TILE, stride=beams), :] = z[:TILE, TILE:] + z[TILE:, :TILE]
-
-    @pl.when(beam == beams - 1)
+    sent[step, :TILE, :] = z[:TILE, :TILE] - z[TILE:, TILE:]
+    sent[step, TILE:, :] = z[:TILE, TILE:] + z[TILE:, :TILE]
+    share(step).start()
+
+    @pl.when(step == steps - 1)
     def _():
+        def place(i, carry):
+            for part, first in ((sent, core * steps), (got, (1 - core) * steps)):
+                at = first + i
+                sr[pl.ds(at, TILE, stride=beams), :] = part[i, :TILE, :]
+                si[pl.ds(at, TILE, stride=beams), :] = part[i, TILE:, :]
+            return carry
+
+        def arrived(i, carry):
+            share(i).wait()
+            return carry
+
+        lax.fori_loop(0, steps, arrived, 0)
+        lax.fori_loop(0, steps, place, 0)
+        spots = spots_ref[my_tile]
         probes = spots.shape[0]
         q = (spots[:, 0:1] + row0) * 1
         r = (spots[:, 1:2] + col0) * 1
@@ -384,8 +427,6 @@
             ei = e[:probes, TILE:] + e[probes:, :TILE]
             return er * er + ei * ei
 
-        own = out_ref.shape[0]
-
         def mine(j, total):
             value = one(ky0 + j)
             out_ref[j] = value
@@ -410,28 +451,23 @@
     length = potential.shape[2]
     beams = beam_tilts.shape[0]
     per_side = CROP // TILE
-    device = lax.axis_index("beam")
     crop_rows = lax.dynamic_slice(potential[1], (0, crop_anchor[1]), (potential.shape[1], CROP))
+    crop_rows = jnp.stack(
+        [crop_rows[:, i * TILE : i * TILE + TILE] for i in range(CROP // TILE)]
+    )
     qh, ql, t1 = forward(potential[0], crop_rows, n, length)
     own = per_side * per_side * TILE // n
-    my_tile = device * own // TILE
-    row0 = crop_anchor[0] + TILE * (my_tile // per_side)
-    col_at = TILE * (my_tile % per_side)
-    col0 = crop_anchor[1] + col_at
-    t1 = lax.dynamic_slice(t1, (row0, col_at), (TILE, TILE))
-    spots = lax.dynamic_slice_in_dim(probe_spots, my_tile, 1, 0)[0]
-    info = jnp.stack((row0, col0, device * own % TILE))
     weights = jnp.concatenate(
         (beam_tilts.T.astype(F32), aperture[None], aberration[None]), 0
     )
     weights = jnp.concatenate((weights,) * 3, 1)
     dh, dl, drow = [jnp.asarray(t) for t in tile_tables()]
-    probes = spots.shape[0]
+    probes = probe_spots.shape[1]
     smem = pl.BlockSpec(memory_space=pltpu.SMEM)
     vmem = pl.BlockSpec(memory_space=pltpu.VMEM)
     return pl.pallas_call(
-        functools.partial(beam_kernel, length, beams),
-        grid=(beams,),
+        functools.partial(beam_kernel, length, beams, n),
+        grid=(beams // 2,),
         out_shape=jax.ShapeDtypeStruct((own, probes, TILE), F32),
         in_specs=[smem, smem] + [vmem] * 8,
         out_specs=vmem,
@@ -441,10 +477,16 @@
             pltpu.VMEM((3 * qh.shape[0], 2 * TILE), BF16),
             pltpu.VMEM((TILE * beams, TILE), F32),
             pltpu.VMEM((TILE * beams, TILE), F32),
+            pltpu.VMEM((beams // 2, 2 * TILE, TILE), F32),
+            pltpu.VMEM((beams // 2, 2 * TILE, TILE), F32),
+            pltpu.SemaphoreType.DMA((beams // 2,)),
+            pltpu.SemaphoreType.DMA((beams // 2,)),
         ],
-        compiler_params=pltpu.CompilerParams(vmem_limit_bytes=LIMIT),
+        compiler_params=pltpu.CompilerParams(
+            collective_id=1, has_side_effects=True, vmem_limit_bytes=LIMIT
+        ),
         name="beams",
-    )(info, beam_tilts.reshape(-1), qh, ql, t1, dh, dl, drow, spots, weights)
+    )(beam_tilts, crop_anchor, qh, ql, t1, dh, dl, drow, probe_spots, weights)
 
 
 def solution(mesh):

time: 91.5 us -> 78.4 us (0.86); the launches traced: 90.1 us -> 78.1 us
  Pallas kernels: 78 us -> 65.9 us
  between operations: 3.5 us -> 1.97 us
  other arithmetic: 1.3 us -> 2.75 us
    pallas_call x1, Pallas kernels: 41.1 us -> 30 us  [per_device(): pl.pallas_call(functools.partial(beam_kernel, length, beams, n), grid=(be...]
    unnamed x9 -> x3, local copies, waits for them, and re-layouts: 0.77 us -> 4.63 us
    dynamic_slice x1 -> x0, local copies, waits for them, and re-layouts: 1.61 us -> none  [per_device(): t1 = lax.dynamic_slice(t1, (row0, col_at), (TILE, TILE))]
    pallas_call x1, Pallas kernels: 37 us -> 35.9 us  [forward(): pl.pallas_call(functools.partial(forward_kernel, n, remote), out_shape=ou...]
where the time goes in v2:
time: 78.4 us; the launch traced here: 78.1 us
  Pallas kernels  65.9 us (84%)
  local copies, waits for them, and re-layouts  7.46 us (10%)
  other arithmetic  2.75 us (4%)
  between operations  1.97 us (3%)
    pallas_call x1, Pallas kernels, forward(): pl.pallas_call(functools.partial(forward_kernel, n, remote), out_shape=ou...  35.9 us
    pallas_call x1, Pallas kernels, per_device(): pl.pallas_call(functools.partial(beam_kernel, length, beams, n), grid=(be...  30 us
    unnamed x3, local copies, waits for them, and re-layouts  4.63 us

profile of v2, /device:TPU:0, one launch (start us, length us, event | category | flops | bytes accessed | tf_op | source)
XLA Modules:
  0.0 78.1 jit_solution(17920024480204551802)
XLA Ops:
  0.0 1.2 %slice.17 = s32[1]{0:T(128)} slice(s32[2]{0:T(128)} %anchor.1), slice={[1:2]} | slice | bytes 8 | tf_op jit(solution)/shard_map/slice | solution.py:454
  3.2 0.7 convert_bitcast_fusion
  3.9 1.4 %maximum_maximum_fusion.weights = f32[4,48]{1,0:T(4,128)} fusion(f32[1,16]{1,0:T(1,128)} %bitcast.13, f32[1,16]{1,0:T(1,128)} %bitcast.14, f32[2,16]{1,0:T(2,128)S(1)} %convert_bitcast_fusion), kind=kLoop, calls=%fused_computation.5 | loop fusion | flops 1536 | bytes 1024 | tf_op jit(solution)/shard_map/concatenate | solution.py:463
  5.3 1.3 %copy.14.tilts = s32[16,2]{1,0:T(8,128)} copy(s32[16,2]{0,1:T(2,128)} %param.14) | data formatting | bytes 256 | tf_op args[1]
  6.7 1.4 %copy.15.spots_ref = s32[4,32,2]{2,1,0:T(8,128)} copy(s32[4,32,2]{1,2,0:T(2,128)} %param.17) | data formatting | bytes 2048 | tf_op args[4]
  8.1 1.5 %fusion = (f32[1,32,512]{2,1,0:T(8,128)S(1)}, f32[32,512]{1,0:T(8,128)}) fusion(f32[2,32,512]{2,1,0:T(8,128)} %param.13), kind=kLoop, calls=%fused_computation.7 | loop fusion | bytes 262144 | tf_op jit(solution)/shard_map/slice | solution.py:454
  9.6 0.1 dynamic-slice_bitcast_fusion
  9.7 0.6 pad_maximum_fusion.crop_ref
  10.3 35.9 %forward.1 = (bf16[384,768]{1,0:T(8,128)(2,1)}, bf16[384,768]{1,0:T(8,128)(2,1)}, f32[512,128]{1,0:T(8,128)}) custom-call(f32[32,512]{1,0:T(8,128)} %get-tuple-element.12.own_ref, f32[2,32,128]{2,1,0:T(8,128)} %pad_maximum_fusion.crop_ref, bf16[1024,768]{1,0:T(8,128)(2,1)} %constant.19.clone.ch_any, bf16[1024,768]{1,0:T(8,128)(2,1)} %constant.20.clone.cl_any, ...), custom_call_target="tpu_custom_call" | custom-call | tf_op jit(solution)/shard_map/forward/pallas_call | solution.py:275
  46.2 30.0 %beams.1 = f32[32,32,128]{2,1,0:T(8,128)} custom-call(s32[16,2]{1,0:T(8,128)} %copy.14.tilts, s32[2]{0:T(128)} %anchor.1, bf16[384,768]{1,0:T(8,128)(2,1)} %get-tuple-element.8.qh_ref, bf16[384,768]{1,0:T(8,128)(2,1)} %get-tuple-element.9.ql_ref, f32[512,128]{1,0:T(8,128)} %get-tuple-element.10.t1_ref, bf16[256,256]{1,0:T(8,128)(2,1)} %constant.23.clone.dh, ...), custom_call_target="tpu_custom_call" | custom-call | tf_op jit(solution)/shard_map/beams/pallas_call | solution.py:468
  76.2 1.9 %copy.17 = f32[32,32,128]{2,1,0:T(8,128)} copy(f32[32,32,128]{2,1,0:T(8,128)} %beams.1) | data formatting | bytes 1048576
  (1 shorter events, 0.0 us)

commit v3 on v2

--- a/solution.py
+++ b/solution.py
@@ -11,6 +11,7 @@
 CROP = 256
 TILE = 128
 MAX_TILT = 16
+BATCH = 4
 F32 = jnp.float32
 BF16 = jnp.bfloat16
 MESH = pl.DeviceIdType.MESH
@@ -89,10 +90,10 @@
 
 
 def forward_kernel(
-    n, remote, own_ref, crop_ref, ch_any, cl_any, rh_any, rl_any, qh_ref, ql_ref, *rest
+    n, remote, own_ref, ch_any, cl_any, rh_any, rl_any, qh_ref, ql_ref, *rest
 ):
     if remote:
-        t1_ref, buf, buf1, ch, cl, rh, rl, th, tl, uh, ul, tab_sem, s0, r0, s1, r1 = rest
+        t1_ref, buf, ch, cl, rh, rl, th, tl, uh, ul, tab_sem, send_sem, recv_sem = rest
     else:
         ch, cl, rh, rl, th, tl, uh, ul, tab_sem = rest
     pairs = ((ch_any, ch), (cl_any, cl), (rh_any, rh), (rl_any, rl))
@@ -115,7 +116,7 @@
         tl[pl.ds(row, count), length:] = l
 
     if remote:
-        rows = own_ref.shape[0]
+        rows = own_ref.shape[1]
         groups = lax.axis_index("groups")
         me = lax.axis_index("beam")
         planes = n // 4
@@ -132,75 +133,61 @@
             pl.semaphore_signal(barrier, inc=1, device_id=(groups, friend), device_id_type=MESH)
         pl.semaphore_wait(barrier, len(friends))
 
-        def push(which, src, block, target, send_index):
-            dst, ss, rs = ((buf, s0, r0), (buf1, s1, r1))[which]
+        def push(src, block, target, index):
             return pltpu.make_async_remote_copy(
                 src_ref=src,
-                dst_ref=dst.at[block],
-                send_sem=ss.at[send_index],
-                recv_sem=rs.at[block],
+                dst_ref=buf.at[block],
+                send_sem=send_sem.at[index],
+                recv_sem=recv_sem.at[block],
                 device_id=(groups, target),
                 device_id_type=MESH,
             )
 
-        def own_part(which, target):
-            return own_ref if which == 0 else crop_ref.at[(target // 4) % (CROP // TILE)]
+        def own_part(target):
+            return own_ref.at[(target // 4) % (CROP // TILE)]
 
         started = []
 
-        def go(which, src, block, target, index):
-            copy = push(which, src, block, target, index)
+        def go(src, block, target):
+            copy = push(src, block, target, len(started))
             copy.start()
             started.append(copy)
 
-        def arrive(which, block):
-            push(which, own_part(which, me), block, sibling, 0).wait_recv()
-
-        order = [1, planes - 1] + [s for s in range(2, planes - 1)]
+        def arrive(block):
+            push(own_part(me), block, sibling, 0).wait_recv()
+
+        def work(block, ref):
+            at = pl.multiple_of(block * rows, rows)
+            transmit(ref[:, :length], at, rows)
+            t1_ref[pl.ds(at, rows), :] = ref[:, length:]
+
+        order = [1, planes - 1] + list(range(2, planes - 1))
         order = [s for i, s in enumerate(order) if s not in order[:i]]
-
-        def open_round(which):
-            go(which, own_part(which, me), me, across, 0)
-            for i, step in enumerate(order):
-                go(which, own_part(which, peer(step)), me, peer(step), 1 + i)
-            go(which, own_part(which, me), me, sibling, planes)
-
-        def forward_round(which, work):
-            dst = (buf, buf1)[which]
-            index = planes + 1
-            work(me, own_part(which, me))
-            for step in [0] + order:
-                base = ((plane + step) % planes) * 4
-                if step != 0:
-                    block = base + low
-                    arrive(which, block)
-                    go(which, dst.at[block], block, across, index)
-                    go(which, dst.at[block], block, sibling, index + 1)
-                    index += 2
-                    work(block, dst.at[block])
-                block = base + (low + 2) % 4
-                arrive(which, block)
-                go(which, dst.at[block], block, sibling, index)
-                index += 1
-                work(block, dst.at[block])
-            for step in [0] + order:
-                base = ((plane + step) % planes) * 4
-                for block in (
-                    base + (low // 2) * 2 + (1 - low % 2),
-                    base + (1 - low // 2) * 2 + (1 - low % 2),
-                ):
-                    arrive(which, block)
-                    work(block, dst.at[block])
-
-        def work0(block, ref):
-            transmit(ref[...], pl.multiple_of(block * rows, rows), rows)
-
-        def work1(block, ref):
-            t1_ref[pl.ds(pl.multiple_of(block * rows, rows), rows), :] = ref[...]
-
-        open_round(0)
-        open_round(1)
-        forward_round(0, work0)
+        go(own_part(me), me, across)
+        for step in order:
+            go(own_part(peer(step)), me, peer(step))
+        go(own_part(me), me, sibling)
+        work(me, own_part(me))
+        for step in [0] + order:
+            base = ((plane + step) % planes) * 4
+            if step != 0:
+                block = base + low
+                arrive(block)
+                go(buf.at[block], block, across)
+                go(buf.at[block], block, sibling)
+                work(block, buf.at[block])
+            block = base + (low + 2) % 4
+            arrive(block)
+            go(buf.at[block], block, sibling)
+            work(block, buf.at[block])
+        for step in [0] + order:
+            base = ((plane + step) % planes) * 4
+            for block in (
+                base + (low // 2) * 2 + (1 - low % 2),
+                base + (1 - low // 2) * 2 + (1 - low % 2),
+            ):
+                arrive(block)
+                work(block, buf.at[block])
     else:
         transmit(own_ref[...], 0, length)
 
@@ -220,8 +207,6 @@
         return carry
 
     lax.fori_loop(0, length // step_rows, stage_one, 0)
-    if remote:
-        forward_round(1, work1)
     for j in range(band // 128):
         a, b = slice(j * 128, j * 128 + 128), slice(band + j * 128, band + j * 128 + 128)
         h = jnp.concatenate((uh[:, a], uh[:, b]), 1)
@@ -262,10 +247,11 @@
     if remote:
         outs = outs + [jax.ShapeDtypeStruct((length, TILE), F32)]
         scratch = (
-            [pltpu.VMEM((n, rows, length), F32), pltpu.VMEM((n, rows, TILE), F32)]
+            [pltpu.VMEM((n, rows, length + TILE), F32)]
             + scratch
-            + [pltpu.SemaphoreType.DMA((n,))] * 4
+            + [pltpu.SemaphoreType.DMA((n,))] * 2
         )
+        own = jnp.stack([jnp.concatenate((own, part), 1) for part in crop])
         params = pltpu.CompilerParams(
             collective_id=0, has_side_effects=True, vmem_limit_bytes=LIMIT
         )
@@ -275,12 +261,12 @@
     result = pl.pallas_call(
         functools.partial(forward_kernel, n, remote),
         out_shape=outs,
-        in_specs=[vmem, vmem] + [pl.BlockSpec(memory_space=pl.ANY)] * 4,
+        in_specs=[vmem] + [pl.BlockSpec(memory_space=pl.ANY)] * 4,
         out_specs=[vmem] * len(outs),
         scratch_shapes=scratch,
         compiler_params=params,
         name="forward",
-    )(own, crop, *tables)
+    )(own, *tables)
     if remote:
         return result
     tile = lax.axis_index("beam") * (CROP // TILE) ** 2 // n
@@ -301,7 +287,7 @@
 
 def beam_kernel(
     length, beams, n, tilts, anchor, qh_ref, ql_ref, t1_ref, dh, dl, drow, spots_ref, weights,
-    out_ref, tr, ti, gcat, sr, si, sent, got, send_sem, recv_sem,
+    out_ref, coef, tr, ti, gcat, sr, si, sent, got, send_sem, recv_sem,
 ):
     step = pl.program_id(0)
     steps = beams // 2
@@ -319,7 +305,7 @@
     col0 = anchor[1] + col_at
     band = qh_ref.shape[0]
     half = band // 2
-    ty, tx = tilts[beam, 0], tilts[beam, 1]
+    ty, tx = tilts[0, beam], tilts[1, beam]
     period = 2 * length
 
     def share(at):
@@ -416,27 +402,41 @@
         full = jnp.concatenate((c * amp, s * amp), 0)
         h = full.astype(BF16).astype(F32)
         lane = lax.broadcasted_iota(jnp.int32, full.shape, 1)
-        coef = jnp.where(lane < 2 * beams, h, full - h).astype(BF16)
-
-        def one(ky):
-            at = pl.multiple_of(ky * beams, beams)
-            both = jnp.concatenate((sr[pl.ds(at, beams), :], si[pl.ds(at, beams), :]), 1)
+        mixed = jnp.where(lane < 2 * BATCH * beams, h, full - h)
+        slot = lax.rem(lax.div(lane, beams), BATCH)
+        for i in range(BATCH):
+            coef[2 * probes * i : 2 * probes * (i + 1), :] = jnp.where(
+                slot == i, mixed, 0.0
+            ).astype(BF16)
+
+        def several(ky):
+            at = pl.multiple_of(ky * beams, BATCH * beams)
+            count = BATCH * beams
+            both = jnp.concatenate((sr[pl.ds(at, count), :], si[pl.ds(at, count), :]), 1)
             h, l = split(both)
-            e = mm(coef, jnp.concatenate((h, l, h), 0))
-            er = e[:probes, :TILE] - e[probes:, TILE:]
-            ei = e[:probes, TILE:] + e[probes:, :TILE]
-            return er * er + ei * ei
+            e = mm(coef[...], jnp.concatenate((h, l, h), 0))
+            found = []
+            for i in range(BATCH):
+                a = e[2 * probes * i : 2 * probes * i + probes]
+                b = e[2 * probes * i + probes : 2 * probes * (i + 1)]
+                er = a[:, :TILE] - b[:, TILE:]
+                ei = a[:, TILE:] + b[:, :TILE]
+                found.append(er * er + ei * ei)
+            return found
 
         def mine(j, total):
-            value = one(ky0 + j)
-            out_ref[j] = value
-            return total + value
+            values = several(ky0 + j * BATCH)
+            for i, value in enumerate(values):
+                out_ref[j * BATCH + i] = value
+            return total + ((values[0] + values[1]) + (values[2] + values[3]))
 
         def others(j, total):
-            return total + one((ky0 + own + j) & (TILE - 1))
-
-        total = lax.fori_loop(0, own, mine, jnp.zeros((probes, TILE), F32), unroll=4)
-        total = lax.fori_loop(0, TILE - own, others, total, unroll=4)
+            values = several((ky0 + own + j * BATCH) & (TILE - 1))
+            return total + ((values[0] + values[1]) + (values[2] + values[3]))
+
+        total = jnp.zeros((probes, TILE), F32)
+        total = lax.fori_loop(0, own // BATCH, mine, total, unroll=min(4, own // BATCH))
+        total = lax.fori_loop(0, (TILE - own) // BATCH, others, total, unroll=4)
         level = jnp.sum(total, axis=1, keepdims=True) * (1.0 / (TILE * TILE))
         scale = 1.0 / (level + 1e-06)
 
@@ -460,7 +460,7 @@
     weights = jnp.concatenate(
         (beam_tilts.T.astype(F32), aperture[None], aberration[None]), 0
     )
-    weights = jnp.concatenate((weights,) * 3, 1)
+    weights = jnp.concatenate((weights,) * (3 * BATCH), 1)
     dh, dl, drow = [jnp.asarray(t) for t in tile_tables()]
     probes = probe_spots.shape[1]
     smem = pl.BlockSpec(memory_space=pltpu.SMEM)
@@ -472,6 +472,7 @@
         in_specs=[smem, smem] + [vmem] * 8,
         out_specs=vmem,
         scratch_shapes=[
+            pltpu.VMEM((2 * BATCH * probes, 3 * BATCH * beams), BF16),
             pltpu.VMEM((TILE, TILE), F32),
             pltpu.VMEM((TILE, TILE), F32),
             pltpu.VMEM((3 * qh.shape[0], 2 * TILE), BF16),
@@ -486,7 +487,7 @@
             collective_id=1, has_side_effects=True, vmem_limit_bytes=LIMIT
         ),
         name="beams",
-    )(beam_tilts, crop_anchor, qh, ql, t1, dh, dl, drow, probe_spots, weights)
+    )(beam_tilts.T, crop_anchor, qh, ql, t1, dh, dl, drow, probe_spots, weights)
 
 
 def solution(mesh):

time: 78.4 us -> 65.6 us (0.84)
  Pallas kernels: 65.9 us -> 55 us
  local copies, waits for them, and re-layouts: 7.46 us -> 6.17 us
    pallas_call x1, Pallas kernels: 35.9 us -> 28.8 us  [forward(): pl.pallas_call(functools.partial(forward_kernel, n, remote), out_shape=ou...]
    pallas_call x1, Pallas kernels: 30 us -> 26.2 us  [per_device(): pl.pallas_call(functools.partial(beam_kernel, length, beams, n), grid=(be...]
    unnamed x3 -> x2, local copies, waits for them, and re-layouts: 4.63 us -> 3.27 us
where the time goes in v3:
time: 65.6 us; the launch traced here: 65.2 us
  Pallas kernels  55 us (84%)
  local copies, waits for them, and re-layouts  6.17 us (9%)
  other arithmetic  2.06 us (3%)
  between operations  1.98 us (3%)
    pallas_call x1, Pallas kernels, forward(): pl.pallas_call(functools.partial(forward_kernel, n, remote), out_shape=ou...  28.8 us
    pallas_call x1, Pallas kernels, per_device(): pl.pallas_call(functools.partial(beam_kernel, length, beams, n), grid=(be...  26.2 us
    unnamed x2, local copies, waits for them, and re-layouts  3.27 us

profile of v3, /device:TPU:0, one launch (start us, length us, event | category | flops | bytes accessed | tf_op | source)
XLA Modules:
  0.0 65.2 jit_solution(226361221803314899)
XLA Ops:
  0.0 1.2 %slice.17 = s32[1]{0:T(128)} slice(s32[2]{0:T(128)} %anchor.1), slice={[1:2]} | slice | bytes 8 | tf_op jit(solution)/shard_map/slice | solution.py:454
  3.2 0.7 %bitcast_convert_fusion = f32[2,16]{1,0:T(2,128)S(1)} fusion(s32[16,2]{0,1:T(2,128)} %param.14), kind=kLoop, calls=%fused_computation.8 | loop fusion | flops 32 | bytes 256 | tf_op jit(solution)/shard_map/convert_element_type | solution.py:461
  3.9 0.7 %pad_maximum_fusion.3 = f32[4,16]{1,0:T(4,128)S(1)} fusion(f32[1,16]{1,0:T(1,128)} %bitcast.14, f32[1,16]{1,0:T(1,128)} %bitcast.15, f32[2,16]{1,0:T(2,128)S(1)} %bitcast_convert_fusion), kind=kLoop, calls=%fused_computation.7 | loop fusion | flops 128 | bytes 512 | tf_op jit(solution)/shard_map/concatenate | solution.py:460
  4.5 0.7 %concatenate.15.weights = f32[4,192]{1,0:T(4,128)} concatenate(f32[4,16]{1,0:T(4,128)S(1)} %pad_maximum_fusion.3, f32[4,16]{1,0:T(4,128)S(1)} %pad_maximum_fusion.3, f32[4,16]{1,0:T(4,128)S(1)} %pad_maximum_fusion.3, f32[4,16]{1,0:T(4,128)S(1)} %pad_maximum_fusion.3, f32[4,16]{1,0:T(4,128)S(1)} %pad_maximum_fusion.3, f32[4,16]{1,0:T(4,128)S(1)} %pad_maximum_fusion.3, ...), dimensions={1} | concatenate | bytes 6144 | tf_op jit(solution)/shard_map/concatenate | solution.py:463
  5.2 1.4 %copy.14.spots_ref = s32[4,32,2]{2,1,0:T(8,128)} copy(s32[4,32,2]{1,2,0:T(2,128)} %param.17) | data formatting | bytes 2048 | tf_op args[4]
  6.6 0.9 %fusion.2 = (f32[1,32,512]{2,1,0:T(8,128)S(1)}, f32[32,512]{1,0:T(8,128)S(1)}) fusion(f32[2,32,512]{2,1,0:T(8,128)} %param.13), kind=kLoop, calls=%fused_computation.9 | loop fusion | bytes 262144 | tf_op jit(solution)/shard_map/slice | solution.py:454
  7.5 0.1 dynamic-slice_bitcast_fusion
  7.6 0.7 %pad_maximum_fusion.own_ref = f32[2,32,640]{2,1,0:T(8,128)} fusion(f32[1,32,640]{2,1,0:T(8,128)S(1)} %get-tuple-element.14, f32[1,32,640]{2,1,0:T(8,128)S(1)} %get-tuple-element.13), kind=kLoop, calls=%fused_computation | loop fusion | flops 40960 | bytes 327680 | tf_op jit(solution)/shard_map/stack | solution.py:254
  8.3 28.8 %forward.1 = (bf16[384,768]{1,0:T(8,128)(2,1)}, bf16[384,768]{1,0:T(8,128)(2,1)}, f32[512,128]{1,0:T(8,128)}) custom-call(f32[2,32,640]{2,1,0:T(8,128)} %pad_maximum_fusion.own_ref, bf16[1024,768]{1,0:T(8,128)(2,1)} %constant.19.clone.ch_any, bf16[1024,768]{1,0:T(8,128)(2,1)} %constant.20.clone.cl_any, bf16[384,512]{1,0:T(8,128)(2,1)} %constant.21.clone.rh_any, ...), custom_call_target="tpu_custom_call" | custom-call | tf_op jit(solution)/shard_map/forward/pallas_call | solution.py:261
  37.1 26.2 %beams.1 = f32[32,32,128]{2,1,0:T(8,128)} custom-call(s32[2,16]{1,0:T(2,128)} %bitcast.13, s32[2]{0:T(128)} %anchor.1, bf16[384,768]{1,0:T(8,128)(2,1)} %get-tuple-element.8.qh_ref, bf16[384,768]{1,0:T(8,128)(2,1)} %get-tuple-element.9.ql_ref, f32[512,128]{1,0:T(8,128)} %get-tuple-element.10.t1_ref, bf16[256,256]{1,0:T(8,128)(2,1)} %constant.23.clone.dh, ...), custom_call_target="tpu_custom_call" | custom-call | tf_op jit(solution)/shard_map/beams/pallas_call | solution.py:468
  63.4 1.9 %copy.16 = f32[32,32,128]{2,1,0:T(8,128)} copy(f32[32,32,128]{2,1,0:T(8,128)} %beams.1) | data formatting | bytes 1048576
  (2 shorter events, 0.0 us)

commit v4 on v3

--- a/solution.py
+++ b/solution.py
@@ -12,6 +12,7 @@
 TILE = 128
 MAX_TILT = 16
 BATCH = 4
+PAIR = 2
 F32 = jnp.float32
 BF16 = jnp.bfloat16
 MESH = pl.DeviceIdType.MESH
@@ -287,7 +288,7 @@
 
 def beam_kernel(
     length, beams, n, tilts, anchor, qh_ref, ql_ref, t1_ref, dh, dl, drow, spots_ref, weights,
-    out_ref, coef, tr, ti, gcat, sr, si, sent, got, send_sem, recv_sem,
+    out_ref, coef, tr, ti, gcats, sr, si, sent, got, send_sem, recv_sem,
 ):
     step = pl.program_id(0)
     steps = beams // 2
@@ -295,7 +296,6 @@
     me = lax.axis_index("beam")
     core = me % 2
     sibling = me + 1 - 2 * core
-    beam = core * steps + step
     own = out_ref.shape[0]
     per_side = CROP // TILE
     my_tile = me * own // TILE
@@ -305,7 +305,6 @@
     col0 = anchor[1] + col_at
     band = qh_ref.shape[0]
     half = band // 2
-    ty, tx = tilts[0, beam], tilts[1, beam]
     period = 2 * length
 
     def share(at):
@@ -327,56 +326,62 @@
         tr[...] = c
         ti[...] = s
 
-    f = lax.broadcasted_iota(jnp.int32, (band, TILE), 0) - half + tx
-    cell = lax.broadcasted_iota(jnp.int32, (band, TILE), 1) + col0
-    c, s = cos_sin_int(f * (2 * cell - f), period)
-    chi, clo = split(c)
-    shi, slo = split(s)
-    xh = jnp.concatenate(
-        (jnp.concatenate((chi, shi), 1), jnp.concatenate((-shi, chi), 1)), 0
-    )
-    xl = jnp.concatenate(
-        (jnp.concatenate((clo, slo), 1), jnp.concatenate((-slo, clo), 1)), 0
-    )
-    k = lax.broadcasted_iota(jnp.int32, (TILE, band), 1)
-    f = jnp.where(k < half, k, half - k) + ty
-    cell = lax.broadcasted_iota(jnp.int32, (TILE, band), 0) + row0
-    c, s = cos_sin_int(f * (2 * cell - f), period)
-    c = jnp.where(k == half, 0.0, c)
-    s = jnp.where(k == half, 0.0, s)
-    chi, clo = split(c)
-    shi, slo = split(s)
-    yh = jnp.concatenate((chi, shi), 0)
-    yl = jnp.concatenate((clo, slo), 0)
-
-    fx = (lax.broadcasted_iota(jnp.int32, (1, band), 1) - half + tx).astype(F32)
-    fx2 = 9.0 * fx * fx
-    k = lax.broadcasted_iota(jnp.int32, (band, 1), 0)
-    fy = (jnp.where(k < half, k, half - k) + ty).astype(F32)
-    keep = jnp.where(9.0 * fy * fy + fx2 < float(length * length), 1.0, 0.0).astype(BF16)
-    keep = jnp.concatenate((keep, keep), 1)
-    h = qh_ref[...] * keep
-    l = ql_ref[...] * keep
-    both = mm(jnp.concatenate((h, l), 0), xh)
-    g = both[:band] + both[band:] + mm(h, xl)
-    gh, gl = split(g)
-    gcat[:band, :] = gh
-    gcat[band : 2 * band, :] = gl
-    gcat[2 * band :, :] = gh
-    p = mm(jnp.concatenate((yh, yh, yl), 1), gcat[...])
-    wr = p[:TILE, :TILE] - p[TILE:, TILE:]
-    wi = p[:TILE, TILE:] + p[TILE:, :TILE]
-    a, b = tr[...], ti[...]
-    w = jnp.concatenate((wr * a - wi * b, wr * b + wi * a), 1)
-    h, l = split(w)
-    v = mm(h, dh[...]) + mm(l, dh[...]) + mm(h, dl[...])
-    h, l = split(v)
-    z = mm(drow[...], jnp.concatenate((h, l, h), 0))
-    sent[step, :TILE, :] = z[:TILE, :TILE] - z[TILE:, TILE:]
-    sent[step, TILE:, :] = z[:TILE, TILE:] + z[TILE:, :TILE]
-    share(step).start()
-
-    @pl.when(step == steps - 1)
+    def one_beam(index, gcat):
+        beam = core * steps + index
+        ty, tx = tilts[0, beam], tilts[1, beam]
+        f = lax.broadcasted_iota(jnp.int32, (band, TILE), 0) - half + tx
+        cell = lax.broadcasted_iota(jnp.int32, (band, TILE), 1) + col0
+        c, s = cos_sin_int(f * (2 * cell - f), period)
+        chi, clo = split(c)
+        shi, slo = split(s)
+        xh = jnp.concatenate(
+            (jnp.concatenate((chi, shi), 1), jnp.concatenate((-shi, chi), 1)), 0
+        )
+        xl = jnp.concatenate(
+            (jnp.concatenate((clo, slo), 1), jnp.concatenate((-slo, clo), 1)), 0
+        )
+        k = lax.broadcasted_iota(jnp.int32, (TILE, band), 1)
+        f = jnp.where(k < half, k, half - k) + ty
+        cell = lax.broadcasted_iota(jnp.int32, (TILE, band), 0) + row0
+        c, s = cos_sin_int(f * (2 * cell - f), period)
+        c = jnp.where(k == half, 0.0, c)
+        s = jnp.where(k == half, 0.0, s)
+        chi, clo = split(c)
+        shi, slo = split(s)
+        yh = jnp.concatenate((chi, shi), 0)
+        yl = jnp.concatenate((clo, slo), 0)
+
+        fx = (lax.broadcasted_iota(jnp.int32, (1, band), 1) - half + tx).astype(F32)
+        fx2 = 9.0 * fx * fx
+        k = lax.broadcasted_iota(jnp.int32, (band, 1), 0)
+        fy = (jnp.where(k < half, k, half - k) + ty).astype(F32)
+        keep = jnp.where(9.0 * fy * fy + fx2 < float(length * length), 1.0, 0.0).astype(BF16)
+        keep = jnp.concatenate((keep, keep), 1)
+        h = qh_ref[...] * keep
+        l = ql_ref[...] * keep
+        both = mm(jnp.concatenate((h, l), 0), xh)
+        g = both[:band] + both[band:] + mm(h, xl)
+        gh, gl = split(g)
+        gcat[:band, :] = gh
+        gcat[band : 2 * band, :] = gl
+        gcat[2 * band :, :] = gh
+        p = mm(jnp.concatenate((yh, yh, yl), 1), gcat[...])
+        wr = p[:TILE, :TILE] - p[TILE:, TILE:]
+        wi = p[:TILE, TILE:] + p[TILE:, :TILE]
+        a, b = tr[...], ti[...]
+        w = jnp.concatenate((wr * a - wi * b, wr * b + wi * a), 1)
+        h, l = split(w)
+        v = mm(h, dh[...]) + mm(l, dh[...]) + mm(h, dl[...])
+        h, l = split(v)
+        z = mm(drow[...], jnp.concatenate((h, l, h), 0))
+        sent[index, :TILE, :] = z[:TILE, :TILE] - z[TILE:, TILE:]
+        sent[index, TILE:, :] = z[:TILE, TILE:] + z[TILE:, :TILE]
+        share(index).start()
+
+    for i in range(PAIR):
+        one_beam(step * PAIR + i, gcats.at[i])
+
+    @pl.when(step == steps // PAIR - 1)
     def _():
         def place(i, carry):
             for part, first in ((sent, core * steps), (got, (1 - core) * steps)):
@@ -391,10 +396,18 @@
 
         lax.fori_loop(0, steps, arrived, 0)
         lax.fori_loop(0, steps, place, 0)
-        spots = spots_ref[my_tile]
-        probes = spots.shape[0]
-        q = (spots[:, 0:1] + row0) * 1
-        r = (spots[:, 1:2] + col0) * 1
+        spots = spots_ref[my_tile].astype(F32)
+        probes = spots.shape[1]
+        eye = lax.broadcasted_iota(jnp.int32, (probes, probes), 0) == lax.broadcasted_iota(
+            jnp.int32, (probes, probes), 1
+        )
+
+        def column(line):
+            picked = jnp.where(eye, jnp.broadcast_to(line, (probes, probes)), 0.0)
+            return jnp.sum(picked, axis=1, keepdims=True).astype(jnp.int32)
+
+        q = column(spots[0:1, :]) + row0
+        r = column(spots[1:2, :]) + col0
         phase = weights[0:1, :].astype(jnp.int32) * q + weights[1:2, :].astype(jnp.int32) * r
         phase = (phase & (length - 1)).astype(F32)
         c, s = cos_sin(weights[3:4, :] - phase * (2.0 * np.pi / length))
@@ -467,7 +480,7 @@
     vmem = pl.BlockSpec(memory_space=pltpu.VMEM)
     return pl.pallas_call(
         functools.partial(beam_kernel, length, beams, n),
-        grid=(beams // 2,),
+        grid=(beams // 2 // PAIR,),
         out_shape=jax.ShapeDtypeStruct((own, probes, TILE), F32),
         in_specs=[smem, smem] + [vmem] * 8,
         out_specs=vmem,
@@ -475,7 +488,7 @@
             pltpu.VMEM((2 * BATCH * probes, 3 * BATCH * beams), BF16),
             pltpu.VMEM((TILE, TILE), F32),
             pltpu.VMEM((TILE, TILE), F32),
-            pltpu.VMEM((3 * qh.shape[0], 2 * TILE), BF16),
+            pltpu.VMEM((PAIR, 3 * qh.shape[0], 2 * TILE), BF16),
             pltpu.VMEM((TILE * beams, TILE), F32),
             pltpu.VMEM((TILE * beams, TILE), F32),
             pltpu.VMEM((beams // 2, 2 * TILE, TILE), F32),
@@ -487,7 +500,7 @@
             collective_id=1, has_side_effects=True, vmem_limit_bytes=LIMIT
         ),
         name="beams",
-    )(beam_tilts.T, crop_anchor, qh, ql, t1, dh, dl, drow, probe_spots, weights)
+    )(beam_tilts.T, crop_anchor, qh, ql, t1, dh, dl, drow, probe_spots.swapaxes(1, 2), weights)
 
 
 def solution(mesh):

time: 65.6 us -> 64.3 us (0.980)
  local copies, waits for them, and re-layouts: 6.17 us -> 4.76 us
    unnamed x2 -> x1, local copies, waits for them, and re-layouts: 3.27 us -> 1.87 us
where the time goes in v4:
time: 64.3 us; the launch traced here: 64 us
  Pallas kernels  55.2 us (86%)
  local copies, waits for them, and re-layouts  4.76 us (7%)
  other arithmetic  2.06 us (3%)
  between operations  1.98 us (3%)
    pallas_call x1, Pallas kernels, forward(): pl.pallas_call(functools.partial(forward_kernel, n, remote), out_shape=ou...  28.8 us
    pallas_call x1, Pallas kernels, per_device(): pl.pallas_call(functools.partial(beam_kernel, length, beams, n), grid=(be...  26.4 us
    unnamed x1, local copies, waits for them, and re-layouts  1.87 us

profile of v4, /device:TPU:0, one launch (start us, length us, event | category | flops | bytes accessed | tf_op | source)
XLA Modules:
  0.0 64.0 jit_solution(14899204373094347069)
XLA Ops:
  0.0 1.2 %slice.17 = s32[1]{0:T(128)} slice(s32[2]{0:T(128)} %anchor.1), slice={[1:2]} | slice | bytes 8 | tf_op jit(solution)/shard_map/slice | solution.py:467
  3.2 0.7 %bitcast_convert_fusion = f32[2,16]{1,0:T(2,128)S(1)} fusion(s32[16,2]{0,1:T(2,128)} %param.14), kind=kLoop, calls=%fused_computation.8 | loop fusion | flops 32 | bytes 256 | tf_op jit(solution)/shard_map/convert_element_type | solution.py:474
  3.9 0.7 %pad_maximum_fusion.3 = f32[4,16]{1,0:T(4,128)S(1)} fusion(f32[1,16]{1,0:T(1,128)} %bitcast.16, f32[1,16]{1,0:T(1,128)} %bitcast.17, f32[2,16]{1,0:T(2,128)S(1)} %bitcast_convert_fusion), kind=kLoop, calls=%fused_computation.7 | loop fusion | flops 128 | bytes 512 | tf_op jit(solution)/shard_map/concatenate | solution.py:473
  4.5 0.7 %concatenate.15.weights = f32[4,192]{1,0:T(4,128)} concatenate(f32[4,16]{1,0:T(4,128)S(1)} %pad_maximum_fusion.3, f32[4,16]{1,0:T(4,128)S(1)} %pad_maximum_fusion.3, f32[4,16]{1,0:T(4,128)S(1)} %pad_maximum_fusion.3, f32[4,16]{1,0:T(4,128)S(1)} %pad_maximum_fusion.3, f32[4,16]{1,0:T(4,128)S(1)} %pad_maximum_fusion.3, f32[4,16]{1,0:T(4,128)S(1)} %pad_maximum_fusion.3, ...), dimensions={1} | concatenate | bytes 6144 | tf_op jit(solution)/shard_map/concatenate | solution.py:476
  5.2 0.9 %fusion.2 = (f32[1,32,512]{2,1,0:T(8,128)S(1)}, f32[32,512]{1,0:T(8,128)S(1)}) fusion(f32[2,32,512]{2,1,0:T(8,128)} %param.13), kind=kLoop, calls=%fused_computation.9 | loop fusion | bytes 262144 | tf_op jit(solution)/shard_map/slice | solution.py:467
  6.1 0.1 dynamic-slice_bitcast_fusion
  6.2 0.7 %pad_maximum_fusion.own_ref = f32[2,32,640]{2,1,0:T(8,128)} fusion(f32[1,32,640]{2,1,0:T(8,128)S(1)} %get-tuple-element.14, f32[1,32,640]{2,1,0:T(8,128)S(1)} %get-tuple-element.13), kind=kLoop, calls=%fused_computation | loop fusion | flops 40960 | bytes 327680 | tf_op jit(solution)/shard_map/stack | solution.py:255
  6.9 28.8 %forward.1 = (bf16[384,768]{1,0:T(8,128)(2,1)}, bf16[384,768]{1,0:T(8,128)(2,1)}, f32[512,128]{1,0:T(8,128)}) custom-call(f32[2,32,640]{2,1,0:T(8,128)} %pad_maximum_fusion.own_ref, bf16[1024,768]{1,0:T(8,128)(2,1)} %constant.19.clone.ch_any, bf16[1024,768]{1,0:T(8,128)(2,1)} %constant.20.clone.cl_any, bf16[384,512]{1,0:T(8,128)(2,1)} %constant.21.clone.rh_any, ...), custom_call_target="tpu_custom_call" | custom-call | tf_op jit(solution)/shard_map/forward/pallas_call | solution.py:262
  35.7 26.4 %beams.1 = f32[32,32,128]{2,1,0:T(8,128)} custom-call(s32[2,16]{1,0:T(2,128)} %bitcast.14, s32[2]{0:T(128)} %anchor.1, bf16[384,768]{1,0:T(8,128)(2,1)} %get-tuple-element.8.qh_ref, bf16[384,768]{1,0:T(8,128)(2,1)} %get-tuple-element.9.ql_ref, f32[512,128]{1,0:T(8,128)} %get-tuple-element.10.t1_ref, bf16[256,256]{1,0:T(8,128)(2,1)} %constant.23.clone.dh, ...), custom_call_target="tpu_custom_call" | custom-call | tf_op jit(solution)/shard_map/beams/pallas_call | solution.py:481
  62.1 1.9 %copy.15 = f32[32,32,128]{2,1,0:T(8,128)} copy(f32[32,32,128]{2,1,0:T(8,128)} %beams.1) | data formatting | bytes 1048576
  (2 shorter events, 0.0 us)
